TPU v7x, 32 devices: a whole 2x2x4 slice. The times are simulated.
32 devices in a mesh: seq: 16 (over z, x, core), tensor: 2 (over y).
Axes of the slice: x: 2, y: 2, z: 4, core: 2. Of those that a mesh axis runs over, the one named last changes fastest.
Arguments:
- projected: bfloat16 [3, 4096, 4096], P(None, 'seq', 'tensor'), may hold values from -6 to 6
- feat_weight: float32 [3, 7, 4096], P(None, None, 'tensor'), may hold values from -2 to 2
- long_filter: float32 [4096, 4096], P(('tensor', 'seq')), may hold values from -1.2 to 1.2
- skip_gain: float32 [4096], P(('tensor', 'seq')), may hold values from 0.5 to 1.5
- out_values: bfloat16 [4096, 2048], P('tensor'), may hold values from -0.125 to 0.125
- out_scales: float32 [32, 16], P('tensor'), may hold values from 0.125 to 1
Outputs:
- mixed: bfloat16 [4096, 2048], P('seq', 'tensor')
All inputs are finite; a program needn't handle non-finite values.
Results may differ from a plain program's by a relative error of at most 0.023.
Values may be sent and summed in bfloat16 or wider, within the bound.
A program may use at most 128 MiB of HBM per device.

v0:
```python
import math

import jax
import jax.numpy as jnp
from jax import lax
from jax.sharding import PartitionSpec as P

KS = 7
BLK = 128


TRIPLE = lax.Precision.HIGH


def passed_along(x, axis, by):
    size = lax.axis_size(axis)
    pairs = [(i, i + by) for i in range(size) if 0 <= i + by < size]
    return lax.ppermute(x, axis, pairs)


def split_length(whole):
    for candidate in range(2, whole + 1, 2):
        if whole % candidate == 0 and candidate * candidate >= whole:
            return (candidate, whole // candidate)
    return (whole, 1)


def angle_pair(row_count, col_count, period):
    row_ids = lax.broadcasted_iota(jnp.int32, (row_count, col_count), 0)
    col_ids = lax.broadcasted_iota(jnp.int32, (row_count, col_count), 1)
    angles = (row_ids * col_ids % period).astype(jnp.float32) * (2.0 * math.pi / period)
    return (jnp.cos(angles), jnp.sin(angles))


def make_tables(length):
    whole = 2 * length
    size_a, size_b = split_length(whole)
    return (
        angle_pair(size_a, size_a, size_a),
        angle_pair(size_b, size_b, size_b),
        angle_pair(size_a, size_b, whole),
        size_a,
        size_b,
    )


def right_mul(signal, matrix):
    return jnp.einsum("ckn,nm->ckm", signal, matrix, precision=TRIPLE)


def forward(signal, tables):
    (cos_a, sin_a), (cos_b, sin_b), (cos_t, sin_t), size_a, size_b = tables
    half_a = size_a // 2
    blocks = signal.reshape(signal.shape[0], half_a, size_b)
    real_a = jnp.einsum("kn,cnb->ckb", cos_a[:, :half_a], blocks, precision=TRIPLE)
    imag_a = -jnp.einsum("kn,cnb->ckb", sin_a[:, :half_a], blocks, precision=TRIPLE)
    real_t = real_a * cos_t + imag_a * sin_t
    imag_t = imag_a * cos_t - real_a * sin_t
    real_f = right_mul(real_t, cos_b) + right_mul(imag_t, sin_b)
    imag_f = right_mul(imag_t, cos_b) - right_mul(real_t, sin_b)
    return (real_f, imag_f)


def inverse(real_f, imag_f, tables):
    (cos_a, sin_a), (cos_b, sin_b), (cos_t, sin_t), size_a, size_b = tables
    half_a = size_a // 2
    real_z = right_mul(real_f, cos_b) - right_mul(imag_f, sin_b)
    imag_z = right_mul(imag_f, cos_b) + right_mul(real_f, sin_b)
    real_w = real_z * cos_t - imag_z * sin_t
    imag_w = imag_z * cos_t + real_z * sin_t
    out_half = jnp.einsum("nk,ckb->cnb", cos_a[:half_a, :], real_w, precision=TRIPLE) - jnp.einsum(
        "nk,ckb->cnb", sin_a[:half_a, :], imag_w, precision=TRIPLE
    )
    return out_half.reshape(out_half.shape[0], half_a * size_b) * (1.0 / (size_a * size_b))


def long_mix(gated_kv, spectrum, own_gain, tables):
    kv_values = gated_kv.astype(jnp.float32)
    real_u, imag_u = forward(kv_values, tables)
    real_h, imag_h = spectrum
    real_p = real_u * real_h - imag_u * imag_h
    imag_p = real_u * imag_h + imag_u * real_h
    convolved = inverse(real_p, imag_p, tables)
    return (convolved + own_gain[:, None] * kv_values).astype(jnp.bfloat16)


def featurize(extended, weights, length):
    tap_count = weights.shape[1]
    running = jnp.zeros(extended.shape[:2] + (length,), jnp.float32)
    for lag_idx in range(tap_count):
        offset = tap_count - 1 - lag_idx
        running = running + weights[:, lag_idx, :, None] * extended[
            :, :, offset : offset + length
        ].astype(jnp.float32)
    return running.astype(jnp.bfloat16)


def multiply_round(left_arr, right_arr):
    return (left_arr.astype(jnp.float32) * right_arr.astype(jnp.float32)).astype(jnp.bfloat16)


def local(projected, feat_weight, long_filter, skip_gain, out_values, out_scales):
    groups = lax.axis_size("seq")
    tok_rows = projected.shape[1]
    local_ch = projected.shape[2]
    length = tok_rows * groups
    tables = make_tables(length)
    spectrum = forward(long_filter, tables)
    columns = jnp.transpose(projected, (0, 2, 1))
    rim_width = KS - 1
    prior_rows = passed_along(columns[:, :, tok_rows - rim_width :], "seq", 1)
    featured = featurize(jnp.concatenate([prior_rows, columns], axis=2), feat_weight, tok_rows)
    regrouped = lax.all_to_all(featured, "seq", split_axis=1, concat_axis=2, tiled=True)
    gated_kv = multiply_round(regrouped[1], regrouped[2])
    filtered = long_mix(gated_kv, spectrum, skip_gain, tables)
    gated = multiply_round(regrouped[0], filtered)
    gated_home = lax.all_to_all(gated, "seq", split_axis=1, concat_axis=0, tiled=True)
    block_count = local_ch // BLK
    out_width = out_values.shape[1]
    stacked = gated_home.reshape(block_count, BLK, tok_rows)
    weight_blocks = out_values.reshape(block_count, BLK, out_width)
    scale_cols = jnp.repeat(out_scales, BLK, axis=1)
    products = jnp.einsum(
        "bkn,bkt->bnt", weight_blocks, stacked, preferred_element_type=jnp.float32
    )
    summed = lax.psum_scatter(
        jnp.sum(products * scale_cols[:, :, None], axis=0).astype(jnp.bfloat16),
        "tensor",
        scatter_dimension=0,
        tiled=True,
    )
    return jnp.transpose(summed, (1, 0))


def solution(mesh):
    return jax.shard_map(
        local,
        mesh=mesh,
        in_specs=(
            P(None, "seq", "tensor"),
            P(None, None, "tensor"),
            P(("tensor", "seq"), None),
            P(("tensor", "seq")),
            P("tensor", None),
            P("tensor", None),
        ),
        out_specs=P("seq", "tensor"),
        check_vma=False,
    )
```

profile of v0, /device:TPU:0, one launch (start us, length us, event | category | flops | bytes accessed | tf_op | source)
XLA Modules:
  0.0 314.8 jit_solution(3486457465249629294)
XLA Ops:
  6.5 0.9 slice.93
  7.5 2.4 collective-permute-start
  9.8 2.1 fusion.149
  12.1 15.2 %add_convert_fusion = bf16[3,2048,256]{1,2,0:T(8,128)(2,1)S(1)} fusion(bf16[3,2048,256]{1,2,0:T(8,128)(2,1)} %bitcast.126, bf16[3,2048,6]{1,2,0:T(8,128)(2,1)S(1)} %collective-permute-done, f32[3,2048]{1,0:T(4,128)S(1)} %get-tuple-element.20, f32[3,2048]{1,0:T(4,128)S(1)} %get-tuple-element.21, f32[3,2048]{1,0:T(4,128)S(1)} %get-tuple-element.22, ...), kind=kLoop, calls=%fused_computation.6 | loop fusion | flops 61341696 | bytes 6537216 | tf_op jit(solution)/shard_map/convert_element_type | solution.py:95
  27.3 4.9 %copy.47 = bf16[3,2048,256]{2,0,1:T(4,128)(2,1)} copy(bf16[3,2048,256]{1,2,0:T(8,128)(2,1)S(1)} %add_convert_fusion) | data formatting | bytes 6291456 | tf_op jit(solution)/shard_map/convert_element_type | solution.py:95
  32.1 9.2 %all-to-all-start = ((bf16[3,2048,256]{2,0,1:T(4,128)(2,1)}), bf16[3,2048,256]{2,0,1:T(4,128)(2,1)}, u32[]{:S(2)}, u32[]{:S(2)}) async-start(bf16[3,2048,256]{2,0,1:T(4,128)(2,1)} %copy.47), calls=%async_computation | async-start | bytes 8388608 | tf_op jit(solution)/shard_map/all_to_all | solution.py:113
  41.4 1.9 copy.54
  43.3 0.3 fusion.82
  43.6 0.3 fusion.81
  43.8 0.1 fusion.99
  44.0 4.9 %fusion.36 = f32[128,128,64]{1,0,2:T(8,128)} fusion(f32[128,64,64]{0,2,1:T(8,128)S(1)} %bitcast.120, f32[128,128]{0,1:T(8,128)S(1)} %fusion.81), kind=kOutput, calls=%fused_computation.59 | convolution fusion | flops 402653184 | bytes 6324224 | tf_op jit(solution)/shard_map/kn,cnb->ckb/dot_general | solution.py:56
  48.9 4.8 %fusion.38 = f32[128,128,64]{1,0,2:T(8,128)} fusion(f32[128,64,64]{0,2,1:T(8,128)S(1)} %bitcast.121, f32[128,128]{0,1:T(8,128)S(1)} %fusion.82), kind=kOutput, calls=%fused_computation.61 | convolution fusion | flops 402653184 | bytes 6324224 | tf_op jit(solution)/shard_map/kn,cnb->ckb/dot_general | solution.py:55
  53.7 65.3 %all-to-all-done = bf16[3,2048,256]{2,0,1:T(4,128)(2,1)} async-done(((bf16[3,2048,256]{2,0,1:T(4,128)(2,1)}), bf16[3,2048,256]{2,0,1:T(4,128)(2,1)}, u32[]{:S(2)}, u32[]{:S(2)}) %all-to-all-start) | async-done | bytes 3145760 | tf_op jit(solution)/shard_map/all_to_all | solution.py:113
  119.0 5.7 %copy.49 = bf16[3,16,128,256]{2,3,1,0:T(8,128)(2,1)S(1)} copy(bf16[3,16,128,256]{3,0,2,1:T(4,128)(2,1)} %bitcast.1) | data formatting | bytes 6291456 | tf_op jit(solution)/shard_map/all_to_all | solution.py:113
  124.8 0.3 multiply_convert_fusion
  125.1 2.0 fusion.43
  127.1 0.2 copy-done.4
  127.4 1.3 copy-done.5
  128.6 8.4 %subtract_bitcast_fusion = (f32[128,128,64]{0,1,2:T(8,128)}, f32[128,128,64]{0,1,2:T(8,128)}, f32[128,128,64]{1,0,2:T(8,128)S(1)}, f32[128,128,64]{1,0,2:T(8,128)}) fusion(f32[128,128,64]{1,0,2:T(8,128)S(1)} %copy-done.5, f32[128,128,64]{1,0,2:T(8,128)S(1)} %copy-done.4, f32[128,64]{0,1:T(8,128)S(1)} %get-tuple-element.26, ...), kind=kOutput, calls=%fused_computation.25 | convolution fusion | flops 417333248 | bytes 30572544 | tf_op jit(solution)/shard_map/kn,cnb->ckb/dot_general | solution.py:55
  137.1 6.2 %fusion.10 = f32[128,128,64]{1,2,0:T(8,128)} fusion(f32[128,128,64]{1,0,2:T(8,128)S(1)} %get-tuple-element.18), kind=kOutput, calls=%fused_computation.27 | convolution fusion | flops 402710528 | bytes 8388608 | tf_op jit(solution)/shard_map/ckn,nm->ckm/dot_general | solution.py:48
  143.3 6.2 %fusion.12 = f32[128,128,64]{1,2,0:T(8,128)} fusion(f32[128,128,64]{1,0,2:T(8,128)S(1)} %get-tuple-element.18), kind=kOutput, calls=%fused_computation.29 | convolution fusion | flops 402710528 | bytes 8388608 | tf_op jit(solution)/shard_map/ckn,nm->ckm/dot_general | solution.py:48
  149.5 5.4 %copy.58 = f32[128,128,64]{1,2,0:T(8,128)} copy(f32[128,128,64]{0,1,2:T(8,128)} %get-tuple-element.7) | data formatting | bytes 8388608 | tf_op jit(solution)/shard_map/sub | solution.py:58
  154.9 5.8 %copy.57 = f32[128,128,64]{1,2,0:T(8,128)} copy(f32[128,128,64]{0,1,2:T(8,128)} %get-tuple-element.8) | data formatting | bytes 8388608 | tf_op jit(solution)/shard_map/add | solution.py:57
  160.7 4.3 %fusion.74 = f32[128,128,64]{1,2,0:T(8,128)S(1)} fusion(f32[128,128,64]{1,2,0:T(8,128)} %copy.57), kind=kOutput, calls=%fused_computation.118 | convolution fusion | flops 402710528 | bytes 8388608 | tf_op jit(solution)/shard_map/ckn,nm->ckm/dot_general | solution.py:48
  165.0 2.0 fusion.71
  167.0 2.1 convolution_add_fusion
  169.1 0.1 copy-done.1
  169.1 3.9 %convolution_subtract_fusion = f32[128,128,64]{1,2,0:T(8,128)} fusion(f32[128,128,64]{1,2,0:T(8,128)S(1)} %fusion.71, f32[128,128,64]{1,2,0:T(8,128)S(1)} %copy-done.1), kind=kOutput, calls=%fused_computation.46 | convolution fusion | flops 403759104 | bytes 12582912 | tf_op jit(solution)/shard_map/ckn,nm->ckm/dot_general | solution.py:48
  173.1 0.7 copy-done.3
  173.8 6.4 %fusion.23 = f32[128,128,64]{1,2,0:T(8,128)} fusion(f32[128,128,64]{1,2,0:T(8,128)S(1)} %copy-done.3, f32[128,128,64]{1,0,2:T(8,128)S(1)} %copy-done), kind=kOutput, calls=%fused_computation.44 | convolution fusion | flops 403759104 | bytes 12582912 | tf_op jit(solution)/shard_map/ckn,nm->ckm/dot_general | solution.py:48
  180.2 10.6 %multiply_subtract_fusion = (f32[128,128,64]{1,2,0:T(8,128)S(1)}, f32[128,128,64]{1,2,0:T(8,128)S(1)}) fusion(f32[128,128,64]{1,2,0:T(8,128)} %convolution_subtract_fusion, f32[128,128,64]{1,2,0:T(8,128)} %fusion.23, f32[128,128,64]{1,2,0:T(8,128)S(1)} %convolution_add_fusion, f32[128,128,64]{1,2,0:T(8,128)} %fusion.10, f32[128,128,64]{1,0,2:T(8,128)S(1)} %copy-done), kind=kOutput, calls=%fused_computation.24 | convolution fusion | flops 410050560 | bytes 29360128 | tf_op jit(solution)/shard_map/ckn,nm->ckm/dot_general | solution.py:48
  190.8 2.0 fusion.59
  192.8 2.0 fusion.69
  194.9 2.0 fusion.67
  196.9 2.0 fusion.61
  198.9 15.6 %fusion.2 = f32[128,64,64]{0,2,1:T(8,128)S(1)} fusion(f32[128,64]{0,1:T(8,128)S(1)} %get-tuple-element.26, f32[128,64]{0,1:T(8,128)S(1)} %get-tuple-element.27, f32[128,128,64]{1,2,0:T(8,128)S(1)} %fusion.61, f32[128,128,64]{1,2,0:T(8,128)S(1)} %fusion.69, f32[128,128,64]{1,2,0:T(8,128)S(1)} %fusion.59, f32[128,128,64]{1,2,0:T(8,128)S(1)} %fusion.67, ...), kind=kOutput, calls=%fused_computation.15 | convolution fusion | flops 407896064 | bytes 19005440 | tf_op jit(solution)/shard_map/nk,ckb->cnb/dot_general | solution.py:71
  214.6 15.7 %multiply_bitcast_fusion = f32[128,64,64]{0,1,2:T(8,128)S(1)} fusion(f32[128,64,64]{0,2,1:T(8,128)S(1)} %fusion.2, f32[128,64]{0,1:T(8,128)S(1)} %get-tuple-element.26, f32[128,64]{0,1:T(8,128)S(1)} %get-tuple-element.27, f32[128,128,64]{1,2,0:T(8,128)S(1)} %fusion.61, f32[128,128,64]{1,2,0:T(8,128)S(1)} %fusion.69, f32[128,128,64]{1,2,0:T(8,128)S(1)} %fusion.59, ...), kind=kOutput, calls=%fused_computation.53 | convolution fusion | flops 408944640 | bytes 21102592 | tf_op jit(solution)/shard_map/nk,ckb->cnb/dot_general | solution.py:71
  230.2 0.0 copy-start.8
  230.3 1.2 copy.69
  231.5 0.0 copy-start.7
  231.5 1.6 fusion.31
  233.1 19.6 %all-to-all-start.1 = ((bf16[128,16,256]{0,2,1:T(8,128)(2,1)}), bf16[128,16,256]{0,2,1:T(8,128)(2,1)S(1)}, u32[]{:S(2)}, u32[]{:S(2)}) async-start(bf16[128,16,256]{0,2,1:T(8,128)(2,1)} %fusion.31), calls=%async_computation.1 | async-start | bytes 2097152 | tf_op jit(solution)/shard_map/all_to_all | solution.py:117
  252.7 0.0 reduce-scatter.2.cloned.1.call-start
  252.8 0.1 broadcast_in_dim.2
  252.9 22.7 %all-to-all-done.1 = bf16[128,16,256]{0,2,1:T(8,128)(2,1)S(1)} async-done(((bf16[128,16,256]{0,2,1:T(8,128)(2,1)}), bf16[128,16,256]{0,2,1:T(8,128)(2,1)S(1)}, u32[]{:S(2)}, u32[]{:S(2)}) %all-to-all-start.1) | async-done | bytes 1048608 | tf_op jit(solution)/shard_map/all_to_all | solution.py:117
  275.7 9.4 %multiply_reduce_fusion = bf16[256,2048]{1,0:T(8,128)(2,1)} fusion(f32[16,2048]{1,0:T(8,128)S(1)} %bitcast.130, bf16[16,128,2048]{2,1,0:T(8,128)(2,1)} %bitcast.131, bf16[128,16,256]{0,2,1:T(8,128)(2,1)S(1)} %all-to-all-done.1), kind=kOutput, calls=%fused_computation | convolution fusion | flops 2163736576 | bytes 10616832 | tf_op jit(solution)/shard_map/bkn,bkt->bnt/dot_general | solution.py:123
  285.1 0.0 reduce-scatter.2.cloned.1.call-update
  285.1 22.7 %reduce-scatter.2.cloned.1.call-done = bf16[1024,256]{0,1:T(8,128)(2,1)} async-done(((bf16[2048,256]{0,1:T(8,128)(2,1)}), bf16[1024,256]{0,1:T(8,128)(2,1)}) %reduce-scatter.2.cloned.1.call-update) | async-done | bytes 524304 | tf_op jit(solution)/shard_map/reduce_scatter | solution.py:126
  (18 shorter events, 0.2 us)
Async XLA Ops:
  7.5 4.6 %collective-permute-start = (bf16[3,2048,6]{1,2,0:T(8,128)(2,1)S(1)}, bf16[3,2048,6]{1,2,0:T(8,128)(2,1)S(1)}, u32[]{:S(2)}, u32[]{:S(2)}) collective-permute-start(bf16[3,2048,6]{1,2,0:T(8,128)(2,1)S(1)} %slice.93), channel_id=1, source_target_pairs={{0,2},{2,4},{4,6},{6,8},{8,10},{10,12},{12,14},{14,16},{16,18},{18... | collective-permute-start | bytes 221192 | tf_op jit(solution)/shard_map/ppermute | solution.py:18
  32.1 86.9 %all-to-all-start = ((bf16[3,2048,256]{2,0,1:T(4,128)(2,1)}), bf16[3,2048,256]{2,0,1:T(4,128)(2,1)}, u32[]{:S(2)}, u32[]{:S(2)}) async-start(bf16[3,2048,256]{2,0,1:T(4,128)(2,1)} %copy.47), calls=%async_computation | async-start | bytes 8388608 | tf_op jit(solution)/shard_map/all_to_all | solution.py:113
  124.8 2.6 copy-start.4
  124.8 3.8 %copy-start.5 = (f32[128,128,64]{1,0,2:T(8,128)S(1)}, f32[128,128,64]{1,0,2:T(8,128)}, u32[]{:S(2)}) copy-start(f32[128,128,64]{1,0,2:T(8,128)} %fusion.38) | copy-start | bytes 12582916
  125.1 2.0 copy-start.6
  160.7 4.3 %copy-start.2 = (f32[128,128,64]{1,2,0:T(8,128)S(1)}, f32[128,128,64]{1,2,0:T(8,128)}, u32[]{:S(2)}) copy-start(f32[128,128,64]{1,2,0:T(8,128)} %copy.58) | copy-start | bytes 12582916
  166.9 2.2 copy-start.1
  169.1 3.9 %copy-start = (f32[128,128,64]{1,0,2:T(8,128)S(1)}, f32[128,128,64]{1,0,2:T(8,128)}, u32[]{:S(2)}) copy-start(f32[128,128,64]{1,0,2:T(8,128)} %get-tuple-element.19) | copy-start | bytes 12582916
  169.1 4.6 %copy-start.3 = (f32[128,128,64]{1,2,0:T(8,128)S(1)}, f32[128,128,64]{1,2,0:T(8,128)}, u32[]{:S(2)}) copy-start(f32[128,128,64]{1,2,0:T(8,128)} %fusion.12) | copy-start | bytes 12582916
  230.2 1.2 copy-start.8
  231.5 21.3 %copy-start.7 = (f32[16,16]{1,0:T(8,128)S(1)}, f32[16,16]{1,0:T(8,128)}, u32[]{:S(2)}) copy-start(f32[16,16]{1,0:T(8,128)} %param.11) | copy-start | bytes 3076
  233.1 42.6 %all-to-all-start.1 = ((bf16[128,16,256]{0,2,1:T(8,128)(2,1)}), bf16[128,16,256]{0,2,1:T(8,128)(2,1)S(1)}, u32[]{:S(2)}, u32[]{:S(2)}) async-start(bf16[128,16,256]{0,2,1:T(8,128)(2,1)} %fusion.31), calls=%async_computation.1 | async-start | bytes 2097152 | tf_op jit(solution)/shard_map/all_to_all | solution.py:117
  252.7 55.0 %reduce-scatter.2.cloned.1.call-start = ((), (), s32[]{:S(2)}) async-start(), calls=%async_computation.3 | async-start | bytes 1572864 | tf_op jit(solution)/shard_map/reduce_scatter | solution.py:126
Sparse Core Ops, SparseCore 0:
  285.2 22.4 reduce-scatter.1
where the time goes:
time: 319 us; the launch traced here: 315 us
  waiting for transfers between devices  111 us (35%)
  matrix products  111 us (35%)
  starting transfers between devices  31.3 us (10%)
  local copies, waits for them, and re-layouts  30.5 us (10%)
  other arithmetic  17.7 us (6%)
  between operations  14 us (4%)
    all_to_all x1, waiting for transfers between devices, local(): lax.all_to_all(featured, 'seq', split_axis=1, concat_axis=2, tiled=True)  65.3 us
    dot_general x12, matrix products, right_mul(): return jnp.einsum('ckn,nm->ckm', signal, matrix, precision=TRIPLE)  49.8 us
    all_to_all x1, waiting for transfers between devices, local(): lax.all_to_all(gated, 'seq', split_axis=1, concat_axis=0, tiled=True)  22.7 us
    reduce_scatter x1, waiting for transfers between devices, local(): lax.psum_scatter(jnp.sum(products * scale_cols[:, :, None], axis=0).astyp...  22.7 us
    all_to_all x1, starting transfers between devices, local(): lax.all_to_all(gated, 'seq', split_axis=1, concat_axis=0, tiled=True)  19.6 us
    dot_general x1, matrix products, inverse(): jnp.einsum('nk,ckb->cnb', cos_a[:half_a, :], real_w, precision=TRIPLE)  15.7 us
    dot_general x1, matrix products, inverse(): jnp.einsum('nk,ckb->cnb', sin_a[:half_a, :], imag_w, precision=TRIPLE)  15.6 us
    convert_element_type x1, other arithmetic, featurize(): return running.astype(jnp.bfloat16)  15.2 us
  transfers between devices with their start and end apart: 4, of which 3 were waited for; matrix products, arithmetic and copies ran while one was open for 5% of the time, Pallas kernels for 0%

commit v1 on v0

--- a/solution.py
+++ b/solution.py
@@ -1,12 +1,396 @@
+import functools
 import math
 
 import jax
 import jax.numpy as jnp
+import ml_dtypes
+import numpy as np
 from jax import lax
+from jax.experimental import pallas as pl
+from jax.experimental.pallas import tpu as pltpu
 from jax.sharding import PartitionSpec as P
 
 KS = 7
 BLK = 128
+LANES = 128
+RIM = 16
+SUB = 16
+CHUNK = 64
+MESH_ID = pl.DeviceIdType.MESH
+BF16 = jnp.bfloat16
+F32 = jnp.float32
+
+
+def dft_tables(groups, rows):
+    whole = 2 * groups * rows
+    kept = groups + 1
+    padded = kept + kept % 2
+    n_a = np.arange(groups)
+    k_a = np.arange(kept)
+    r = np.arange(rows)
+    turns = k_a[:, None, None] * (n_a[None, :, None] * rows + r[None, None, :]) % whole
+    angles = turns * (2.0 * np.pi / whole)
+    parts = np.stack([np.cos(angles), -np.sin(angles)], axis=1)
+    blocks = parts.reshape(kept, 2, groups, rows // SUB, SUB)
+    first = np.zeros((rows // SUB, padded, 2, SUB, groups, SUB))
+    last = np.zeros((rows // SUB, groups, SUB, padded, 2, SUB))
+    weight = np.full((kept,), 2.0 / whole)
+    weight[0] = weight[-1] = 1.0 / whole
+    for lo in range(SUB):
+        cut = blocks[:, :, :, :, lo]
+        first[:, :kept, :, lo, :, lo] = cut.transpose(3, 0, 1, 2)
+        last[:, :, lo, :kept, :, lo] = (cut * weight[:, None, None, None]).transpose(3, 2, 0, 1)
+    first = first.reshape(rows // SUB, padded * 2 * SUB, groups * SUB)
+    last = last.reshape(rows // SUB, groups * SUB, padded * 2 * SUB)
+    inner = (r[:, None] * r[None, :] % rows) * (2.0 * np.pi / rows)
+    cos, sin = np.cos(inner), np.sin(inner)
+    ahead = np.block([[cos, sin], [-sin, cos]])
+    back = np.block([[cos, -sin], [sin, cos]])
+    return [x.astype(ml_dtypes.bfloat16) for x in (first, ahead, back, last)]
+
+
+def dot(a, b):
+    return jnp.dot(a, b, preferred_element_type=F32)
+
+
+def fused_kernel(
+    groups,
+    rows,
+    proj,
+    taps,
+    filt,
+    gain,
+    weights,
+    scales,
+    t_first,
+    t_ahead,
+    t_back,
+    t_last,
+    out,
+    pb,
+    g_out,
+    u_in,
+    v_out,
+    f_in,
+    feat_q,
+    fl,
+    ft,
+    x1,
+    spec,
+    m_first,
+    m_ahead,
+    m_back,
+    m_last,
+    w,
+    gated,
+    part_own,
+    part_out,
+    part_in,
+    loc_sem,
+    halo_sem,
+    send_sem,
+    recv_u,
+    recv_f,
+    recv_p,
+):
+    me = lax.axis_index("seq")
+    mine = lax.axis_index("tensor")
+    other = 1 - mine
+    chunks = rows // CHUNK
+    length = groups * rows
+    half = part_own.shape[1]
+
+    load_k = pltpu.make_async_copy(proj, pb.at[:, pl.ds(RIM, rows)], loc_sem.at[0])
+    load_k.start()
+
+    barrier = pltpu.get_barrier_semaphore()
+
+    @pl.loop(1, groups)
+    def _(step):
+        peer = lax.rem(me + step, groups)
+        pl.semaphore_signal(barrier, inc=1, device_id=(peer, mine), device_id_type=MESH_ID)
+
+    pl.semaphore_signal(barrier, inc=1, device_id=(me, other), device_id_type=MESH_ID)
+    pl.semaphore_wait(barrier, groups)
+
+    halo = pltpu.make_async_remote_copy(
+        src_ref=proj.at[:, pl.ds(rows - RIM, RIM)],
+        dst_ref=pb.at[:, pl.ds(0, RIM)],
+        send_sem=halo_sem.at[0],
+        recv_sem=halo_sem.at[1],
+        device_id=(lax.rem(me + 1, groups), mine),
+        device_id_type=MESH_ID,
+    )
+
+    @pl.when(me < groups - 1)
+    def _():
+        halo.start()
+
+    @pl.when(me == 0)
+    def _():
+        pb[:, 0:RIM, :] = jnp.zeros((pb.shape[0], RIM, pb.shape[2]), BF16)
+
+    load_k.wait()
+    loads = [
+        pltpu.make_async_copy(src, dst, loc_sem.at[1 + i])
+        for i, (src, dst) in enumerate(
+            (
+                (filt, fl),
+                (t_first, m_first),
+                (t_ahead, m_ahead),
+                (t_back, m_back),
+                (t_last, m_last),
+                (weights, w),
+            )
+        )
+    ]
+    for load in loads:
+        load.start()
+
+    def featured(p, q, j):
+        lanes = pl.ds(pl.multiple_of(j * LANES, LANES), LANES)
+        x = pb[p, pl.ds(pl.multiple_of(q * CHUNK, CHUNK), CHUNK + RIM), lanes].astype(F32)
+        run = None
+        for lag in range(KS):
+            term = taps[p, lag : lag + 1, lanes] * x[RIM - lag : RIM - lag + CHUNK]
+            run = term if run is None else run + term
+        return run.astype(BF16)
+
+    def rows_of(q):
+        return pl.ds(pl.multiple_of(q * CHUNK, CHUNK), CHUNK)
+
+    def spread(src, dst, q, recv):
+        @pl.loop(1, groups)
+        def _(step):
+            peer = lax.rem(me + step, groups)
+            pltpu.make_async_remote_copy(
+                src_ref=src.at[peer, rows_of(q)],
+                dst_ref=dst.at[me, rows_of(q)],
+                send_sem=send_sem.at[recv],
+                recv_sem=(recv_u if recv == 0 else recv_f).at[q],
+                device_id=(peer, mine),
+                device_id_type=MESH_ID,
+            ).start()
+
+        dst[me, rows_of(q), :] = src[me, rows_of(q), :]
+
+    def await_chunk(dst, q, sem):
+        view = dst.at[pl.ds(0, groups - 1), rows_of(q)]
+        pltpu.make_async_copy(view, view, sem.at[q]).wait()
+
+    def feature_chunk(q):
+        @pl.loop(0, groups)
+        def _(j):
+            k = featured(1, q, j).astype(F32)
+            v = featured(2, q, j).astype(F32)
+            g_out[j, rows_of(q), :] = (k * v).astype(BF16)
+
+        spread(g_out, u_in, q, 0)
+
+    @pl.loop(1, chunks)
+    def _(q):
+        feature_chunk(q)
+
+    @pl.when(me > 0)
+    def _():
+        halo.wait_recv()
+
+    feature_chunk(0)
+
+    loads[0].wait()
+
+    @pl.loop(0, groups)
+    def _(a):
+        for part in range(rows // LANES):
+            start = pl.multiple_of(a * rows + part * LANES, LANES)
+            ft[a, part * LANES : (part + 1) * LANES, :] = fl[:, pl.ds(start, LANES)].T.astype(BF16)
+
+    for load in loads[1:5]:
+        load.wait()
+
+    slabs = x1.shape[0]
+    pairs = slabs // 4
+
+    def first_stage(src, s):
+        at = pl.ds(pl.multiple_of(s * SUB, SUB), SUB)
+        block = src[:, at, :].reshape(groups * SUB, LANES)
+        x1[:, at, :] = dot(m_first[s], block).astype(BF16).reshape(slabs, SUB, LANES)
+
+    def pair_of(j):
+        left = x1[pl.ds(4 * j, 2)].reshape(2 * rows, LANES)
+        right = x1[pl.ds(4 * j + 2, 2)].reshape(2 * rows, LANES)
+        return jnp.concatenate([left, right], axis=1)
+
+    @pl.loop(0, rows // SUB)
+    def _(s):
+        first_stage(ft, s)
+
+    @pl.loop(0, pairs)
+    def _(j):
+        spec[j] = dot(m_ahead[...], pair_of(j))
+
+    loads[5].wait()
+    cuts = w.shape[1] // BLK
+
+    @pl.loop(0, w.shape[0] // BLK)
+    def _(b):
+        at = pl.ds(pl.multiple_of(b * BLK, BLK), BLK)
+        for n in range(cuts):
+            cols = slice(n * BLK, (n + 1) * BLK)
+            w[at, cols] = (w[at, cols].astype(F32) * scales[b, n]).astype(BF16)
+
+    @pl.loop(0, chunks)
+    def _(q):
+        @pl.loop(0, groups)
+        def _(j):
+            feat_q[j, rows_of(q), :] = featured(0, q, j)
+
+    per_chunk = CHUNK // SUB
+
+    @pl.loop(0, chunks)
+    def _(i):
+        q = lax.rem(i + 1, chunks)
+        await_chunk(u_in, q, recv_u)
+
+        @pl.loop(0, per_chunk)
+        def _(s):
+            first_stage(u_in, q * per_chunk + s)
+
+    @pl.loop(0, pairs)
+    def _(j):
+        values = dot(m_ahead[...], pair_of(j))
+        re_u, im_u = values[:rows], values[rows:]
+        re_h, im_h = spec[j, 0:rows, :], spec[j, rows : 2 * rows, :]
+        product = jnp.concatenate(
+            [re_u * re_h - im_u * im_h, re_u * im_h + im_u * re_h], axis=0
+        ).astype(BF16)
+        z = dot(m_back[...], product).astype(BF16)
+        x1[pl.ds(4 * j, 2)] = z[:, :LANES].reshape(2, rows, LANES)
+        x1[pl.ds(4 * j + 2, 2)] = z[:, LANES:].reshape(2, rows, LANES)
+
+    @pl.loop(0, chunks)
+    def _(q):
+        @pl.loop(0, per_chunk)
+        def _(i):
+            s = q * per_chunk + i
+            at = pl.ds(pl.multiple_of(s * SUB, SUB), SUB)
+            conv = dot(m_last[s], x1[:, at, :].reshape(slabs * SUB, LANES))
+            direct = gain[...] * u_in[:, at, :].reshape(groups * SUB, LANES).astype(F32)
+            v_out[:, at, :] = (conv + direct).astype(BF16).reshape(groups, SUB, LANES)
+
+        spread(v_out, f_in, q, 1)
+
+    def swap(q):
+        return pltpu.make_async_remote_copy(
+            src_ref=part_out.at[rows_of(q)],
+            dst_ref=part_in.at[rows_of(q)],
+            send_sem=send_sem.at[2],
+            recv_sem=recv_p.at[q],
+            device_id=(me, other),
+            device_id_type=MESH_ID,
+        )
+
+    @pl.loop(0, chunks)
+    def _(q):
+        await_chunk(f_in, q, recv_f)
+        for j in range(groups):
+            product = feat_q[j, rows_of(q), :].astype(F32) * f_in[j, rows_of(q), :].astype(F32)
+            gated[:, j * LANES : (j + 1) * LANES] = product.astype(BF16)
+        theirs = pl.ds(pl.multiple_of(other * half, half), half)
+        ours = pl.ds(pl.multiple_of(mine * half, half), half)
+        part_out[rows_of(q), :] = dot(gated[...], w[:, theirs]).astype(BF16)
+        swap(q).start()
+        part_own[rows_of(q), :] = dot(gated[...], w[:, ours]).astype(BF16)
+
+    @pl.loop(0, chunks)
+    def _(q):
+        swap(q).wait_recv()
+        total = part_own[rows_of(q), :].astype(F32) + part_in[rows_of(q), :].astype(F32)
+        out[rows_of(q), :] = total.astype(BF16)
+
+    @pl.when(me < groups - 1)
+    def _():
+        halo.wait_send()
+
+    sent = g_out.at[pl.ds(0, groups - 1)]
+    pltpu.make_async_copy(sent, sent, send_sem.at[0]).wait()
+    sent = v_out.at[pl.ds(0, groups - 1)]
+    pltpu.make_async_copy(sent, sent, send_sem.at[1]).wait()
+    pltpu.make_async_copy(part_out, part_out, send_sem.at[2]).wait()
+
+
+def fused(projected, feat_weight, long_filter, skip_gain, out_values, out_scales):
+    groups = lax.axis_size("seq")
+    rows, local_ch = projected.shape[1:]
+    out_width = out_values.shape[1]
+    half = out_width // 2
+    tables = dft_tables(groups, rows)
+    slabs = tables[0].shape[1] // SUB
+    hbm = pl.BlockSpec(memory_space=pl.ANY)
+    vmem = pl.BlockSpec(memory_space=pltpu.VMEM)
+    smem = pl.BlockSpec(memory_space=pltpu.SMEM)
+    block = pltpu.VMEM((groups, rows, LANES), BF16)
+    chunks = rows // CHUNK
+    return pl.pallas_call(
+        functools.partial(fused_kernel, groups, rows),
+        out_shape=jax.ShapeDtypeStruct((rows, half), BF16),
+        in_specs=[hbm, vmem, hbm, vmem, hbm, smem, hbm, hbm, hbm, hbm],
+        out_specs=vmem,
+        scratch_shapes=[
+            pltpu.VMEM((3, RIM + rows, local_ch), BF16),
+            block,
+            block,
+            block,
+            block,
+            block,
+            pltpu.VMEM(long_filter.shape, F32),
+            block,
+            pltpu.VMEM((slabs, rows, LANES), BF16),
+            pltpu.VMEM((slabs // 4, 2 * rows, 2 * LANES), F32),
+            pltpu.VMEM(tables[0].shape, BF16),
+            pltpu.VMEM(tables[1].shape, BF16),
+            pltpu.VMEM(tables[2].shape, BF16),
+            pltpu.VMEM(tables[3].shape, BF16),
+            pltpu.VMEM(out_values.shape, BF16),
+            pltpu.VMEM((CHUNK, local_ch), BF16),
+            pltpu.VMEM((rows, half), BF16),
+            pltpu.VMEM((rows, half), BF16),
+            pltpu.VMEM((rows, half), BF16),
+            pltpu.SemaphoreType.DMA((7,)),
+            pltpu.SemaphoreType.DMA((2,)),
+            pltpu.SemaphoreType.DMA((3,)),
+            pltpu.SemaphoreType.DMA((chunks,)),
+            pltpu.SemaphoreType.DMA((chunks,)),
+            pltpu.SemaphoreType.DMA((chunks,)),
+        ],
+        compiler_params=pltpu.CompilerParams(
+            collective_id=0, has_side_effects=True, vmem_limit_bytes=58 * 2**20
+        ),
+        cost_estimate=pl.CostEstimate(
+            flops=10 * 10**9, bytes_accessed=32 * 2**20, transcendentals=0
+        ),
+    )(
+        projected,
+        feat_weight,
+        long_filter,
+        skip_gain.reshape(1, -1),
+        out_values,
+        out_scales,
+        *[jnp.asarray(x) for x in tables],
+    )
+
+
+def fits(projected, long_filter, out_values):
+    groups = lax.axis_size("seq")
+    rows, local_ch = projected.shape[1:]
+    return (
+        lax.axis_size("tensor") == 2
+        and long_filter.shape[0] == LANES
+        and local_ch == groups * LANES
+        and rows == 2 * LANES
+        and groups == SUB
+        and out_values.shape[1] % (2 * LANES) == 0
+    )
 
 
 TRIPLE = lax.Precision.HIGH
@@ -100,6 +484,8 @@
 
 
 def local(projected, feat_weight, long_filter, skip_gain, out_values, out_scales):
+    if fits(projected, long_filter, out_values):
+        return fused(projected, feat_weight, long_filter, skip_gain, out_values, out_scales)
     groups = lax.axis_size("seq")
     tok_rows = projected.shape[1]
     local_ch = projected.shape[2]

time: 319 us -> 73.8 us (0.23); the launches traced: 315 us -> 73.6 us
  matrix products: 111 us -> 0 us
  waiting for transfers between devices: 111 us -> 0 us
  Pallas kernels: 0 us -> 71.7 us
  starting transfers between devices: 31.3 us -> 0 us
  local copies, waits for them, and re-layouts: 30.5 us -> 1.87 us
  other arithmetic: 17.7 us -> 0 us
  between operations: 14 us -> 0.01 us
    dot_general x19 -> x0, matrix products: 111 us -> none  [the longest x12 49.8 us: right_mul(): return jnp.einsum('ckn,nm->ckm', signal, matrix, precision=TRIPLE)]
    all_to_all x2 -> x0, waiting for transfers between devices: 88.1 us -> none  [the longest x1 65.3 us: local(): lax.all_to_all(featured, 'seq', split_axis=1, concat_axis=2, tiled=True)]
    pallas_call x0 -> x1, Pallas kernels: none -> 71.7 us  [fused(): pl.pallas_call(functools.partial(fused_kernel, groups, rows), out_shape=j...]
    all_to_all x2 -> x0, starting transfers between devices: 28.9 us -> none  [the longest x1 19.6 us: local(): lax.all_to_all(gated, 'seq', split_axis=1, concat_axis=0, tiled=True)]
    reduce_scatter x1 -> x0, waiting for transfers between devices: 22.7 us -> none  [local(): lax.psum_scatter(jnp.sum(products * scale_cols[:, :, None], axis=0).astyp...]
    convert_element_type x3 -> x0, other arithmetic: 17 us -> none  [the longest x1 15.2 us: featurize(): return running.astype(jnp.bfloat16)]
    add x1 -> x0, local copies, waits for them, and re-layouts: 5.77 us -> none  [forward(): real_t = real_a * cos_t + imag_a * sin_t]
    all_to_all x1 -> x0, local copies, waits for them, and re-layouts: 5.75 us -> none  [local(): lax.all_to_all(featured, 'seq', split_axis=1, concat_axis=2, tiled=True)]
  transfers between devices with their start and end apart: 4 -> 0, of which waited for: 3 -> 0; matrix products, arithmetic and copies ran while one was open for 5% -> 0% of each run, Pallas kernels for 0% -> 0%
where the time goes in v1:
time: 73.8 us; the launch traced here: 73.6 us
  Pallas kernels  71.7 us (97%)
  local copies, waits for them, and re-layouts  1.87 us (3%)
    pallas_call x1, Pallas kernels, fused(): pl.pallas_call(functools.partial(fused_kernel, groups, rows), out_shape=j...  71.7 us
    unnamed x1, local copies, waits for them, and re-layouts  1.87 us

profile of v1, /device:TPU:0, one launch (start us, length us, event | category | flops | bytes accessed | tf_op | source)
XLA Modules:
  0.0 73.6 jit_solution(18154415054958050709)
XLA Ops:
  0.0 71.7 %shard_map.100 = bf16[256,1024]{1,0:T(8,128)(2,1)} custom-call(bf16[3,256,2048]{2,1,0:T(8,128)(2,1)} %proj.1, f32[3,7,2048]{2,1,0:T(8,128)} %taps.1, f32[128,4096]{1,0:T(8,128)} %filt.1, f32[1,128]{1,0:T(1,128)} %bitcast.1, bf16[2048,2048]{1,0:T(8,128)(2,1)} %weights.1, f32[16,16]{1,0:T(8,128)} %scales.1, bf16[16,576,256]{2,1,0:T(8,128)(2,1)} %constant.8.clone.t_first, ...), custom_call_target="tpu_custom_call" | custom-call | flops 10000000000 | bytes 33554432 | tf_op jit(solution)/shard_map/pallas_call | solution.py:334
  71.7 1.9 %copy.12 = bf16[256,1024]{1,0:T(8,128)(2,1)} copy(bf16[256,1024]{1,0:T(8,128)(2,1)} %shard_map.100) | data formatting | bytes 1048576

commit v2 on v1

--- a/solution.py
+++ b/solution.py
@@ -23,25 +23,29 @@
 
 def dft_tables(groups, rows):
     whole = 2 * groups * rows
-    kept = groups + 1
-    padded = kept + kept % 2
+    evens = np.arange(0, groups + 1, 2)
+    odds = np.arange(1, groups + 1, 2)
+    slots = len(evens) + len(evens) % 2
+    k_a = np.zeros((2 * slots,), np.int64)
+    weight = np.zeros((2 * slots,))
+    for base, kept in ((0, evens), (slots, odds)):
+        k_a[base : base + len(kept)] = kept
+        weight[base : base + len(kept)] = np.where(kept % groups == 0, 1.0, 2.0) / whole
     n_a = np.arange(groups)
-    k_a = np.arange(kept)
     r = np.arange(rows)
     turns = k_a[:, None, None] * (n_a[None, :, None] * rows + r[None, None, :]) % whole
     angles = turns * (2.0 * np.pi / whole)
     parts = np.stack([np.cos(angles), -np.sin(angles)], axis=1)
-    blocks = parts.reshape(kept, 2, groups, rows // SUB, SUB)
-    first = np.zeros((rows // SUB, padded, 2, SUB, groups, SUB))
-    last = np.zeros((rows // SUB, groups, SUB, padded, 2, SUB))
-    weight = np.full((kept,), 2.0 / whole)
-    weight[0] = weight[-1] = 1.0 / whole
+    parts = parts * (weight > 0)[:, None, None, None]
+    blocks = parts.reshape(2 * slots, 2, groups, rows // SUB, SUB)
+    first = np.zeros((rows // SUB, 2 * slots, 2, SUB, groups, SUB))
+    last = np.zeros((rows // SUB, groups, SUB, 2 * slots, 2, SUB))
     for lo in range(SUB):
         cut = blocks[:, :, :, :, lo]
-        first[:, :kept, :, lo, :, lo] = cut.transpose(3, 0, 1, 2)
-        last[:, :, lo, :kept, :, lo] = (cut * weight[:, None, None, None]).transpose(3, 2, 0, 1)
-    first = first.reshape(rows // SUB, padded * 2 * SUB, groups * SUB)
-    last = last.reshape(rows // SUB, groups * SUB, padded * 2 * SUB)
+        first[:, :, :, lo, :, lo] = cut.transpose(3, 0, 1, 2)
+        last[:, :, lo, :, :, lo] = (cut * weight[:, None, None, None]).transpose(3, 2, 0, 1)
+    first = first.reshape(rows // SUB, 4 * slots * SUB, groups * SUB)
+    last = last.reshape(rows // SUB, groups * SUB, 4 * slots * SUB)
     inner = (r[:, None] * r[None, :] % rows) * (2.0 * np.pi / rows)
     cos, sin = np.cos(inner), np.sin(inner)
     ahead = np.block([[cos, sin], [-sin, cos]])
@@ -51,6 +55,15 @@
 
 def dot(a, b):
     return jnp.dot(a, b, preferred_element_type=F32)
+
+
+def swapped(x):
+    return pltpu.roll(x, LANES // 2, 1)
+
+
+def side_by_side(left, right):
+    low = lax.broadcasted_iota(jnp.int32, left.shape, 1) < LANES // 2
+    return jnp.where(low, left, right)
 
 
 def fused_kernel(
@@ -70,12 +83,14 @@
     pb,
     g_out,
     u_in,
+    u_wide,
     v_out,
     f_in,
     feat_q,
     fl,
     ft,
     x1,
+    xz,
     spec,
     m_first,
     m_ahead,
@@ -89,48 +104,61 @@
     loc_sem,
     halo_sem,
     send_sem,
-    recv_u,
-    recv_f,
+    recv_sem,
     recv_p,
 ):
     me = lax.axis_index("seq")
     mine = lax.axis_index("tensor")
     other = 1 - mine
-    chunks = rows // CHUNK
-    length = groups * rows
-    half = part_own.shape[1]
-
-    load_k = pltpu.make_async_copy(proj, pb.at[:, pl.ds(RIM, rows)], loc_sem.at[0])
-    load_k.start()
+    packed = rows // 2
+    part = CHUNK // 2
+    chunks = packed // part
+    half = part_own.shape[2]
+
+    load_in = pltpu.make_async_copy(proj, pb.at[:, pl.ds(RIM, rows)], loc_sem.at[0])
+    load_in.start()
+
+    def partner(mask):
+        total = 0
+        bit = 1
+        while bit < groups:
+            mixed = lax.rem(me // bit, 2) + lax.rem(mask // bit, 2)
+            total = total + bit * lax.rem(mixed, 2)
+            bit *= 2
+        return total
 
     barrier = pltpu.get_barrier_semaphore()
 
     @pl.loop(1, groups)
     def _(step):
-        peer = lax.rem(me + step, groups)
-        pl.semaphore_signal(barrier, inc=1, device_id=(peer, mine), device_id_type=MESH_ID)
+        pl.semaphore_signal(
+            barrier, inc=1, device_id=(partner(step), mine), device_id_type=MESH_ID
+        )
 
     pl.semaphore_signal(barrier, inc=1, device_id=(me, other), device_id_type=MESH_ID)
     pl.semaphore_wait(barrier, groups)
 
-    halo = pltpu.make_async_remote_copy(
-        src_ref=proj.at[:, pl.ds(rows - RIM, RIM)],
-        dst_ref=pb.at[:, pl.ds(0, RIM)],
-        send_sem=halo_sem.at[0],
-        recv_sem=halo_sem.at[1],
-        device_id=(lax.rem(me + 1, groups), mine),
-        device_id_type=MESH_ID,
-    )
+    def halo(first, count, slot):
+        return pltpu.make_async_remote_copy(
+            src_ref=proj.at[pl.ds(first, count), pl.ds(rows - RIM, RIM)],
+            dst_ref=pb.at[pl.ds(first, count), pl.ds(0, RIM)],
+            send_sem=halo_sem.at[slot],
+            recv_sem=halo_sem.at[slot + 1],
+            device_id=(lax.rem(me + 1, groups), mine),
+            device_id_type=MESH_ID,
+        )
+
+    halo_kv, halo_q = halo(1, 2, 0), halo(0, 1, 2)
 
     @pl.when(me < groups - 1)
     def _():
-        halo.start()
+        halo_kv.start()
 
     @pl.when(me == 0)
     def _():
         pb[:, 0:RIM, :] = jnp.zeros((pb.shape[0], RIM, pb.shape[2]), BF16)
 
-    load_k.wait()
+    load_in.wait()
     loads = [
         pltpu.make_async_copy(src, dst, loc_sem.at[1 + i])
         for i, (src, dst) in enumerate(
@@ -147,45 +175,55 @@
     for load in loads:
         load.start()
 
-    def featured(p, q, j):
+    def featured(p, start, j):
         lanes = pl.ds(pl.multiple_of(j * LANES, LANES), LANES)
-        x = pb[p, pl.ds(pl.multiple_of(q * CHUNK, CHUNK), CHUNK + RIM), lanes].astype(F32)
+        x = pb[p, pl.ds(pl.multiple_of(start, part), part + RIM), lanes].astype(F32)
         run = None
         for lag in range(KS):
-            term = taps[p, lag : lag + 1, lanes] * x[RIM - lag : RIM - lag + CHUNK]
+            term = taps[p, lag : lag + 1, lanes] * x[RIM - lag : RIM - lag + part]
             run = term if run is None else run + term
         return run.astype(BF16)
 
-    def rows_of(q):
-        return pl.ds(pl.multiple_of(q * CHUNK, CHUNK), CHUNK)
-
-    def spread(src, dst, q, recv):
+    def span(start, count):
+        return pl.ds(pl.multiple_of(start, count), count)
+
+    first_slot = (0, chunks, 2 * chunks, 3 * chunks)
+
+    def spread(src, dst, side, q, count):
+        at = span(q * count, count)
+
         @pl.loop(1, groups)
         def _(step):
-            peer = lax.rem(me + step, groups)
+            peer = partner(groups - step)
             pltpu.make_async_remote_copy(
-                src_ref=src.at[peer, rows_of(q)],
-                dst_ref=dst.at[me, rows_of(q)],
-                send_sem=send_sem.at[recv],
-                recv_sem=(recv_u if recv == 0 else recv_f).at[q],
+                src_ref=src.at[side % 2, peer, at],
+                dst_ref=dst.at[side % 2, me, at],
+                send_sem=send_sem.at[side],
+                recv_sem=recv_sem.at[first_slot[side] + q],
                 device_id=(peer, mine),
                 device_id_type=MESH_ID,
             ).start()
 
-        dst[me, rows_of(q), :] = src[me, rows_of(q), :]
-
-    def await_chunk(dst, q, sem):
-        view = dst.at[pl.ds(0, groups - 1), rows_of(q)]
-        pltpu.make_async_copy(view, view, sem.at[q]).wait()
+        dst[side % 2, me, at, :] = src[side % 2, me, at, :]
+
+    def await_chunk(dst, side, q, count):
+        view = dst.at[side % 2, pl.ds(0, groups - 1), span(q * count, count)]
+        pltpu.make_async_copy(view, view, recv_sem.at[first_slot[side] + q]).wait()
 
     def feature_chunk(q):
+        at = span(q * part, part)
+
         @pl.loop(0, groups)
         def _(j):
-            k = featured(1, q, j).astype(F32)
-            v = featured(2, q, j).astype(F32)
-            g_out[j, rows_of(q), :] = (k * v).astype(BF16)
-
-        spread(g_out, u_in, q, 0)
+            def product(start):
+                k = featured(1, start, j).astype(F32)
+                return k * featured(2, start, j).astype(F32)
+
+            early, late = product(q * part), product(packed + q * part)
+            g_out[0, j, at, :] = side_by_side(early, swapped(late)).astype(BF16)
+            g_out[1, j, at, :] = side_by_side(swapped(early), late).astype(BF16)
+
+        spread(g_out, u_in, 0, q, part)
 
     @pl.loop(1, chunks)
     def _(q):
@@ -193,130 +231,186 @@
 
     @pl.when(me > 0)
     def _():
-        halo.wait_recv()
+        halo_kv.wait_recv()
 
     feature_chunk(0)
+    wide = packed // 2
+
+    @pl.loop(0, 2)
+    def _(q):
+        spread(g_out, u_in, 1, q, wide)
+
+    @pl.when(me < groups - 1)
+    def _():
+        halo_q.start()
 
     loads[0].wait()
 
     @pl.loop(0, groups)
     def _(a):
-        for part in range(rows // LANES):
-            start = pl.multiple_of(a * rows + part * LANES, LANES)
-            ft[a, part * LANES : (part + 1) * LANES, :] = fl[:, pl.ds(start, LANES)].T.astype(BF16)
+        for piece in range(rows // LANES):
+            start = pl.multiple_of(a * rows + piece * LANES, LANES)
+            at = slice(piece * LANES, (piece + 1) * LANES)
+            ft[a, at, :] = fl[:, pl.ds(start, LANES)].T.astype(BF16)
 
     for load in loads[1:5]:
         load.wait()
 
-    slabs = x1.shape[0]
-    pairs = slabs // 4
+    slabs = xz.shape[0]
+    half_slabs = slabs // 2
+    fours = half_slabs // 4
 
     def first_stage(src, s):
-        at = pl.ds(pl.multiple_of(s * SUB, SUB), SUB)
-        block = src[:, at, :].reshape(groups * SUB, LANES)
-        x1[:, at, :] = dot(m_first[s], block).astype(BF16).reshape(slabs, SUB, LANES)
-
-    def pair_of(j):
-        left = x1[pl.ds(4 * j, 2)].reshape(2 * rows, LANES)
-        right = x1[pl.ds(4 * j + 2, 2)].reshape(2 * rows, LANES)
+        block = src[:, span(s * SUB, SUB), :].reshape(groups * SUB, LANES)
+        found = dot(m_first[s], block)
+        return found[: half_slabs * SUB], found[half_slabs * SUB :]
+
+    def pack(side, even, odd):
+        if side == 0:
+            both = side_by_side(even, swapped(odd))
+        else:
+            both = side_by_side(swapped(even), odd)
+        return both.astype(BF16).reshape(half_slabs, SUB, LANES)
+
+    def four_of(src, j):
+        left = src[pl.ds(4 * j, 2)].reshape(2 * rows, LANES)
+        right = src[pl.ds(4 * j + 2, 2)].reshape(2 * rows, LANES)
         return jnp.concatenate([left, right], axis=1)
 
     @pl.loop(0, rows // SUB)
     def _(s):
-        first_stage(ft, s)
-
-    @pl.loop(0, pairs)
+        even, odd = first_stage(ft, s)
+        x1[:, span(s * SUB, SUB), :] = pack(0, even, odd)
+        xz[0:half_slabs, span(s * SUB, SUB), :] = pack(1, even, odd)
+
+    @pl.loop(0, fours)
     def _(j):
-        spec[j] = dot(m_ahead[...], pair_of(j))
+        spec[0, j] = dot(m_ahead[...], four_of(x1, j))
+        spec[1, j] = dot(m_ahead[...], four_of(xz, j))
+
+    def convolve(side, count, back):
+        @pl.loop(0, packed // count)
+        def _(i):
+            q = lax.rem(i + 1, packed // count)
+            await_chunk(u_in, side, q, count)
+            at = span(q * count, count)
+            held = u_in[side, :, at, :].reshape(groups * count, LANES)
+            turned = swapped(held.astype(F32)).astype(BF16)
+            early, late = (held, turned) if side == 0 else (turned, held)
+            u_wide[:, at, :] = early.reshape(groups, count, LANES)
+            u_wide[:, span(packed + q * count, count), :] = late.reshape(groups, count, LANES)
+
+            @pl.loop(0, count // SUB)
+            def _(c):
+                for base in (0, packed // SUB):
+                    s = base + q * (count // SUB) + c
+                    x1[:, span(s * SUB, SUB), :] = pack(side, *first_stage(u_wide, s))
+
+        @pl.loop(0, fours)
+        def _(j):
+            values = dot(m_ahead[...], four_of(x1, j))
+            re_u, im_u = values[:rows], values[rows:]
+            re_h, im_h = spec[side, j, 0:rows, :], spec[side, j, rows : 2 * rows, :]
+            product = jnp.concatenate(
+                [re_u * re_h - im_u * im_h, re_u * im_h + im_u * re_h], axis=0
+            ).astype(BF16)
+            z = dot(m_back[...], product)
+            for piece in range(2):
+                held = z[:, piece * LANES : (piece + 1) * LANES]
+                turned = swapped(held)
+                even, odd = (held, turned) if side == 0 else (turned, held)
+                at = 4 * j + 2 * piece
+                xz[pl.ds(at, 2)] = even.astype(BF16).reshape(2, rows, LANES)
+                xz[pl.ds(half_slabs + at, 2)] = odd.astype(BF16).reshape(2, rows, LANES)
+
+        def filtered(s):
+            at = span(s * SUB, SUB)
+            conv = dot(m_last[s], xz[:, at, :].reshape(slabs * SUB, LANES))
+            direct = gain[...] * u_wide[:, at, :].reshape(groups * SUB, LANES).astype(F32)
+            return conv + direct
+
+        @pl.loop(0, packed // back)
+        def _(q):
+            @pl.loop(0, back // SUB)
+            def _(c):
+                s = q * (back // SUB) + c
+                early, late = filtered(s), filtered(packed // SUB + s)
+                if side == 0:
+                    both = side_by_side(early, swapped(late))
+                else:
+                    both = side_by_side(swapped(early), late)
+                v_out[side, :, span(s * SUB, SUB), :] = both.astype(BF16).reshape(
+                    groups, SUB, LANES
+                )
+
+            spread(v_out, f_in, 2 + side, q, back)
+
+    convolve(0, part, wide)
+    convolve(1, wide, part)
 
     loads[5].wait()
-    cuts = w.shape[1] // BLK
 
     @pl.loop(0, w.shape[0] // BLK)
     def _(b):
-        at = pl.ds(pl.multiple_of(b * BLK, BLK), BLK)
-        for n in range(cuts):
+        at = span(b * BLK, BLK)
+        for n in range(w.shape[1] // BLK):
             cols = slice(n * BLK, (n + 1) * BLK)
             w[at, cols] = (w[at, cols].astype(F32) * scales[b, n]).astype(BF16)
 
-    @pl.loop(0, chunks)
+    @pl.when(me > 0)
+    def _():
+        halo_q.wait_recv()
+
+    @pl.loop(0, rows // part)
     def _(q):
         @pl.loop(0, groups)
         def _(j):
-            feat_q[j, rows_of(q), :] = featured(0, q, j)
-
-    per_chunk = CHUNK // SUB
-
-    @pl.loop(0, chunks)
-    def _(i):
-        q = lax.rem(i + 1, chunks)
-        await_chunk(u_in, q, recv_u)
-
-        @pl.loop(0, per_chunk)
-        def _(s):
-            first_stage(u_in, q * per_chunk + s)
-
-    @pl.loop(0, pairs)
-    def _(j):
-        values = dot(m_ahead[...], pair_of(j))
-        re_u, im_u = values[:rows], values[rows:]
-        re_h, im_h = spec[j, 0:rows, :], spec[j, rows : 2 * rows, :]
-        product = jnp.concatenate(
-            [re_u * re_h - im_u * im_h, re_u * im_h + im_u * re_h], axis=0
-        ).astype(BF16)
-        z = dot(m_back[...], product).astype(BF16)
-        x1[pl.ds(4 * j, 2)] = z[:, :LANES].reshape(2, rows, LANES)
-        x1[pl.ds(4 * j + 2, 2)] = z[:, LANES:].reshape(2, rows, LANES)
-
-    @pl.loop(0, chunks)
-    def _(q):
-        @pl.loop(0, per_chunk)
-        def _(i):
-            s = q * per_chunk + i
-            at = pl.ds(pl.multiple_of(s * SUB, SUB), SUB)
-            conv = dot(m_last[s], x1[:, at, :].reshape(slabs * SUB, LANES))
-            direct = gain[...] * u_in[:, at, :].reshape(groups * SUB, LANES).astype(F32)
-            v_out[:, at, :] = (conv + direct).astype(BF16).reshape(groups, SUB, LANES)
-
-        spread(v_out, f_in, q, 1)
+            feat_q[j, span(q * part, part), :] = featured(0, q * part, j)
 
     def swap(q):
         return pltpu.make_async_remote_copy(
-            src_ref=part_out.at[rows_of(q)],
-            dst_ref=part_in.at[rows_of(q)],
-            send_sem=send_sem.at[2],
+            src_ref=part_out.at[q],
+            dst_ref=part_in.at[q],
+            send_sem=send_sem.at[4],
             recv_sem=recv_p.at[q],
             device_id=(me, other),
             device_id_type=MESH_ID,
         )
 
+    for q in range(packed // wide):
+        await_chunk(f_in, 2, q, wide)
+
     @pl.loop(0, chunks)
     def _(q):
-        await_chunk(f_in, q, recv_f)
+        await_chunk(f_in, 3, q, part)
+        at, later = span(q * part, part), span(packed + q * part, part)
         for j in range(groups):
-            product = feat_q[j, rows_of(q), :].astype(F32) * f_in[j, rows_of(q), :].astype(F32)
-            gated[:, j * LANES : (j + 1) * LANES] = product.astype(BF16)
-        theirs = pl.ds(pl.multiple_of(other * half, half), half)
-        ours = pl.ds(pl.multiple_of(mine * half, half), half)
-        part_out[rows_of(q), :] = dot(gated[...], w[:, theirs]).astype(BF16)
+            lanes = slice(j * LANES, (j + 1) * LANES)
+            low, high = f_in[0, j, at, :].astype(F32), f_in[1, j, at, :].astype(F32)
+            early = side_by_side(low, swapped(high)) * feat_q[j, at, :].astype(F32)
+            late = side_by_side(swapped(low), high) * feat_q[j, later, :].astype(F32)
+            gated[0:part, lanes] = early.astype(BF16)
+            gated[part : 2 * part, lanes] = late.astype(BF16)
+        part_out[q] = dot(gated[...], w[:, span(other * half, half)]).astype(BF16)
         swap(q).start()
-        part_own[rows_of(q), :] = dot(gated[...], w[:, ours]).astype(BF16)
+        part_own[q] = dot(gated[...], w[:, span(mine * half, half)]).astype(BF16)
 
     @pl.loop(0, chunks)
     def _(q):
         swap(q).wait_recv()
-        total = part_own[rows_of(q), :].astype(F32) + part_in[rows_of(q), :].astype(F32)
-        out[rows_of(q), :] = total.astype(BF16)
+        total = (part_own[q].astype(F32) + part_in[q].astype(F32)).astype(BF16)
+        out[span(q * part, part), :] = total[:part]
+        out[span(packed + q * part, part), :] = total[part:]
 
     @pl.when(me < groups - 1)
     def _():
-        halo.wait_send()
-
-    sent = g_out.at[pl.ds(0, groups - 1)]
-    pltpu.make_async_copy(sent, sent, send_sem.at[0]).wait()
-    sent = v_out.at[pl.ds(0, groups - 1)]
-    pltpu.make_async_copy(sent, sent, send_sem.at[1]).wait()
-    pltpu.make_async_copy(part_out, part_out, send_sem.at[2]).wait()
+        halo_kv.wait_send()
+        halo_q.wait_send()
+
+    for side in range(4):
+        sent = (g_out if side < 2 else v_out).at[side % 2, pl.ds(0, groups - 1)]
+        pltpu.make_async_copy(sent, sent, send_sem.at[side]).wait()
+    pltpu.make_async_copy(part_out, part_out, send_sem.at[4]).wait()
 
 
 def fused(projected, feat_weight, long_filter, skip_gain, out_values, out_scales):
@@ -330,6 +424,7 @@
     vmem = pl.BlockSpec(memory_space=pltpu.VMEM)
     smem = pl.BlockSpec(memory_space=pltpu.SMEM)
     block = pltpu.VMEM((groups, rows, LANES), BF16)
+    halves = pltpu.VMEM((2, groups, rows // 2, LANES), BF16)
     chunks = rows // CHUNK
     return pl.pallas_call(
         functools.partial(fused_kernel, groups, rows),
@@ -338,29 +433,30 @@
         out_specs=vmem,
         scratch_shapes=[
             pltpu.VMEM((3, RIM + rows, local_ch), BF16),
+            halves,
+            halves,
             block,
-            block,
-            block,
-            block,
+            halves,
+            halves,
             block,
             pltpu.VMEM(long_filter.shape, F32),
             block,
+            pltpu.VMEM((slabs // 2, rows, LANES), BF16),
             pltpu.VMEM((slabs, rows, LANES), BF16),
-            pltpu.VMEM((slabs // 4, 2 * rows, 2 * LANES), F32),
+            pltpu.VMEM((2, slabs // 8, 2 * rows, 2 * LANES), F32),
             pltpu.VMEM(tables[0].shape, BF16),
             pltpu.VMEM(tables[1].shape, BF16),
             pltpu.VMEM(tables[2].shape, BF16),
             pltpu.VMEM(tables[3].shape, BF16),
             pltpu.VMEM(out_values.shape, BF16),
             pltpu.VMEM((CHUNK, local_ch), BF16),
-            pltpu.VMEM((rows, half), BF16),
-            pltpu.VMEM((rows, half), BF16),
-            pltpu.VMEM((rows, half), BF16),
+            pltpu.VMEM((chunks, CHUNK, half), BF16),
+            pltpu.VMEM((chunks, CHUNK, half), BF16),
+            pltpu.VMEM((chunks, CHUNK, half), BF16),
             pltpu.SemaphoreType.DMA((7,)),
-            pltpu.SemaphoreType.DMA((2,)),
-            pltpu.SemaphoreType.DMA((3,)),
-            pltpu.SemaphoreType.DMA((chunks,)),
-            pltpu.SemaphoreType.DMA((chunks,)),
+            pltpu.SemaphoreType.DMA((4,)),
+            pltpu.SemaphoreType.DMA((5,)),
+            pltpu.SemaphoreType.DMA((4 * chunks,)),
             pltpu.SemaphoreType.DMA((chunks,)),
         ],
         compiler_params=pltpu.CompilerParams(

time: 73.8 us -> 77.4 us (1.049)
  Pallas kernels: 71.7 us -> 75.3 us
    pallas_call x1, Pallas kernels: 71.7 us -> 75.3 us  [fused(): pl.pallas_call(functools.partial(fused_kernel, groups, rows), out_shape=j...]
where the time goes in v2:
time: 77.4 us; the launch traced here: 77.2 us
  Pallas kernels  75.3 us (97%)
  local copies, waits for them, and re-layouts  1.87 us (2%)
    pallas_call x1, Pallas kernels, fused(): pl.pallas_call(functools.partial(fused_kernel, groups, rows), out_shape=j...  75.3 us
    unnamed x1, local copies, waits for them, and re-layouts  1.87 us

profile of v2, /device:TPU:0, one launch (start us, length us, event | category | flops | bytes accessed | tf_op | source)
XLA Modules:
  0.0 77.2 jit_solution(11345569802680141165)
XLA Ops:
  0.0 75.3 %shard_map.100 = bf16[256,1024]{1,0:T(8,128)(2,1)} custom-call(bf16[3,256,2048]{2,1,0:T(8,128)(2,1)} %proj.1, f32[3,7,2048]{2,1,0:T(8,128)} %taps.1, f32[128,4096]{1,0:T(8,128)} %filt.1, f32[1,128]{1,0:T(1,128)} %bitcast.1, bf16[2048,2048]{1,0:T(8,128)(2,1)} %weights.1, f32[16,16]{1,0:T(8,128)} %scales.1, bf16[16,640,256]{2,1,0:T(8,128)(2,1)} %constant.8.clone.t_first, ...), custom_call_target="tpu_custom_call" | custom-call | flops 10000000000 | bytes 33554432 | tf_op jit(solution)/shard_map/pallas_call | solution.py:429
  75.3 1.9 %copy.12 = bf16[256,1024]{1,0:T(8,128)(2,1)} copy(bf16[256,1024]{1,0:T(8,128)(2,1)} %shard_map.100) | data formatting | bytes 1048576

commit v3 on v2

--- a/solution.py
+++ b/solution.py
@@ -246,7 +246,7 @@
 
     loads[0].wait()
 
-    @pl.loop(0, groups)
+    @pl.loop(0, groups, unroll=4)
     def _(a):
         for piece in range(rows // LANES):
             start = pl.multiple_of(a * rows + piece * LANES, LANES)
@@ -277,14 +277,13 @@
         right = src[pl.ds(4 * j + 2, 2)].reshape(2 * rows, LANES)
         return jnp.concatenate([left, right], axis=1)
 
-    @pl.loop(0, rows // SUB)
+    @pl.loop(0, rows // SUB, unroll=4)
     def _(s):
         even, odd = first_stage(ft, s)
         x1[:, span(s * SUB, SUB), :] = pack(0, even, odd)
         xz[0:half_slabs, span(s * SUB, SUB), :] = pack(1, even, odd)
 
-    @pl.loop(0, fours)
-    def _(j):
+    for j in range(fours):
         spec[0, j] = dot(m_ahead[...], four_of(x1, j))
         spec[1, j] = dot(m_ahead[...], four_of(xz, j))
 
@@ -300,14 +299,13 @@
             u_wide[:, at, :] = early.reshape(groups, count, LANES)
             u_wide[:, span(packed + q * count, count), :] = late.reshape(groups, count, LANES)
 
-            @pl.loop(0, count // SUB)
+            @pl.loop(0, count // SUB, unroll=2)
             def _(c):
                 for base in (0, packed // SUB):
                     s = base + q * (count // SUB) + c
                     x1[:, span(s * SUB, SUB), :] = pack(side, *first_stage(u_wide, s))
 
-        @pl.loop(0, fours)
-        def _(j):
+        for j in range(fours):
             values = dot(m_ahead[...], four_of(x1, j))
             re_u, im_u = values[:rows], values[rows:]
             re_h, im_h = spec[side, j, 0:rows, :], spec[side, j, rows : 2 * rows, :]
@@ -331,7 +329,7 @@
 
         @pl.loop(0, packed // back)
         def _(q):
-            @pl.loop(0, back // SUB)
+            @pl.loop(0, back // SUB, unroll=2)
             def _(c):
                 s = q * (back // SUB) + c
                 early, late = filtered(s), filtered(packed // SUB + s)
@@ -363,7 +361,7 @@
 
     @pl.loop(0, rows // part)
     def _(q):
-        @pl.loop(0, groups)
+        @pl.loop(0, groups, unroll=4)
         def _(j):
             feat_q[j, span(q * part, part), :] = featured(0, q * part, j)
 

time: 77.4 us -> 69.1 us (0.89)
  Pallas kernels: 75.3 us -> 67 us
    pallas_call x1, Pallas kernels: 75.3 us -> 67 us  [fused(): pl.pallas_call(functools.partial(fused_kernel, groups, rows), out_shape=j...]
where the time goes in v3:
time: 69.1 us; the launch traced here: 68.9 us
  Pallas kernels  67 us (97%)
  local copies, waits for them, and re-layouts  1.87 us (3%)
    pallas_call x1, Pallas kernels, fused(): pl.pallas_call(functools.partial(fused_kernel, groups, rows), out_shape=j...  67 us
    unnamed x1, local copies, waits for them, and re-layouts  1.87 us

profile of v3, /device:TPU:0, one launch (start us, length us, event | category | flops | bytes accessed | tf_op | source)
XLA Modules:
  0.0 68.9 jit_solution(13783580598586096326)
XLA Ops:
  0.0 67.0 %shard_map.100 = bf16[256,1024]{1,0:T(8,128)(2,1)} custom-call(bf16[3,256,2048]{2,1,0:T(8,128)(2,1)} %proj.1, f32[3,7,2048]{2,1,0:T(8,128)} %taps.1, f32[128,4096]{1,0:T(8,128)} %filt.1, f32[1,128]{1,0:T(1,128)} %bitcast.1, bf16[2048,2048]{1,0:T(8,128)(2,1)} %weights.1, f32[16,16]{1,0:T(8,128)} %scales.1, bf16[16,640,256]{2,1,0:T(8,128)(2,1)} %constant.8.clone.t_first, ...), custom_call_target="tpu_custom_call" | custom-call | flops 10000000000 | bytes 33554432 | tf_op jit(solution)/shard_map/pallas_call | solution.py:427
  67.1 1.9 %copy.12 = bf16[256,1024]{1,0:T(8,128)(2,1)} copy(bf16[256,1024]{1,0:T(8,128)(2,1)} %shard_map.100) | data formatting | bytes 1048576

commit v4 on v3

--- a/solution.py
+++ b/solution.py
@@ -210,6 +210,8 @@
         view = dst.at[side % 2, pl.ds(0, groups - 1), span(q * count, count)]
         pltpu.make_async_copy(view, view, recv_sem.at[first_slot[side] + q]).wait()
 
+    wide = packed // 2
+
     def feature_chunk(q):
         at = span(q * part, part)
 
@@ -223,22 +225,18 @@
             g_out[0, j, at, :] = side_by_side(early, swapped(late)).astype(BF16)
             g_out[1, j, at, :] = side_by_side(swapped(early), late).astype(BF16)
 
-        spread(g_out, u_in, 0, q, part)
-
-    @pl.loop(1, chunks)
-    def _(q):
-        feature_chunk(q)
+    feature_chunk(chunks - 2)
+    feature_chunk(chunks - 1)
+    spread(g_out, u_in, 0, 1, wide)
+    feature_chunk(1)
 
     @pl.when(me > 0)
     def _():
         halo_kv.wait_recv()
 
     feature_chunk(0)
-    wide = packed // 2
-
-    @pl.loop(0, 2)
-    def _(q):
-        spread(g_out, u_in, 1, q, wide)
+    spread(g_out, u_in, 0, 0, wide)
+    spread(g_out, u_in, 1, 0, packed)
 
     @pl.when(me < groups - 1)
     def _():
@@ -251,7 +249,7 @@
         for piece in range(rows // LANES):
             start = pl.multiple_of(a * rows + piece * LANES, LANES)
             at = slice(piece * LANES, (piece + 1) * LANES)
-            ft[a, at, :] = fl[:, pl.ds(start, LANES)].T.astype(BF16)
+            ft[a, at, :] = fl[:, pl.ds(start, LANES)].astype(BF16).T
 
     for load in loads[1:5]:
         load.wait()
@@ -293,11 +291,14 @@
             q = lax.rem(i + 1, packed // count)
             await_chunk(u_in, side, q, count)
             at = span(q * count, count)
-            held = u_in[side, :, at, :].reshape(groups * count, LANES)
-            turned = swapped(held.astype(F32)).astype(BF16)
-            early, late = (held, turned) if side == 0 else (turned, held)
-            u_wide[:, at, :] = early.reshape(groups, count, LANES)
-            u_wide[:, span(packed + q * count, count), :] = late.reshape(groups, count, LANES)
+
+            @pl.loop(0, groups, unroll=4)
+            def _(a):
+                held = u_in[side, a, at, :]
+                turned = swapped(held.astype(F32)).astype(BF16)
+                early, late = (held, turned) if side == 0 else (turned, held)
+                u_wide[a, at, :] = early
+                u_wide[a, span(packed + q * count, count), :] = late
 
             @pl.loop(0, count // SUB, unroll=2)
             def _(c):
@@ -329,7 +330,7 @@
 
         @pl.loop(0, packed // back)
         def _(q):
-            @pl.loop(0, back // SUB, unroll=2)
+            @pl.loop(0, back // SUB, unroll=min(4, back // SUB))
             def _(c):
                 s = q * (back // SUB) + c
                 early, late = filtered(s), filtered(packed // SUB + s)
@@ -343,8 +344,8 @@
 
             spread(v_out, f_in, 2 + side, q, back)
 
-    convolve(0, part, wide)
-    convolve(1, wide, part)
+    convolve(0, wide, packed)
+    convolve(1, packed, part)
 
     loads[5].wait()
 
@@ -353,7 +354,8 @@
         at = span(b * BLK, BLK)
         for n in range(w.shape[1] // BLK):
             cols = slice(n * BLK, (n + 1) * BLK)
-            w[at, cols] = (w[at, cols].astype(F32) * scales[b, n]).astype(BF16)
+            scale = jnp.full((BLK, BLK), scales[b, n], F32).astype(BF16)
+            w[at, cols] = w[at, cols] * scale
 
     @pl.when(me > 0)
     def _():
@@ -375,8 +377,7 @@
             device_id_type=MESH_ID,
         )
 
-    for q in range(packed // wide):
-        await_chunk(f_in, 2, q, wide)
+    await_chunk(f_in, 2, 0, packed)
 
     @pl.loop(0, chunks)
     def _(q):

time: 69.1 us -> 70.6 us (1.022)
  Pallas kernels: 67 us -> 68.5 us
    pallas_call x1, Pallas kernels: 67 us -> 68.5 us  [fused(): pl.pallas_call(functools.partial(fused_kernel, groups, rows), out_shape=j...]
where the time goes in v4:
time: 70.6 us; the launch traced here: 70.4 us
  Pallas kernels  68.5 us (97%)
  local copies, waits for them, and re-layouts  1.87 us (3%)
    pallas_call x1, Pallas kernels, fused(): pl.pallas_call(functools.partial(fused_kernel, groups, rows), out_shape=j...  68.5 us
    unnamed x1, local copies, waits for them, and re-layouts  1.87 us

profile of v4, /device:TPU:0, one launch (start us, length us, event | category | flops | bytes accessed | tf_op | source)
XLA Modules:
  0.0 70.4 jit_solution(11883257003703968755)
XLA Ops:
  0.0 68.5 %shard_map.100 = bf16[256,1024]{1,0:T(8,128)(2,1)} custom-call(bf16[3,256,2048]{2,1,0:T(8,128)(2,1)} %proj.1, f32[3,7,2048]{2,1,0:T(8,128)} %taps.1, f32[128,4096]{1,0:T(8,128)} %filt.1, f32[1,128]{1,0:T(1,128)} %bitcast.1, bf16[2048,2048]{1,0:T(8,128)(2,1)} %weights.1, f32[16,16]{1,0:T(8,128)} %scales.1, bf16[16,640,256]{2,1,0:T(8,128)(2,1)} %constant.8.clone.t_first, ...), custom_call_target="tpu_custom_call" | custom-call | flops 10000000000 | bytes 33554432 | tf_op jit(solution)/shard_map/pallas_call | solution.py:428
  68.5 1.9 %copy.12 = bf16[256,1024]{1,0:T(8,128)(2,1)} copy(bf16[256,1024]{1,0:T(8,128)(2,1)} %shard_map.100) | data formatting | bytes 1048576

commit v5 on v4

--- a/solution.py
+++ b/solution.py
@@ -194,7 +194,8 @@
 
         @pl.loop(1, groups)
         def _(step):
-            peer = partner(groups - step)
+            across = lax.rem(step, 2)
+            peer = partner(across * (groups // 2) + step // 2)
             pltpu.make_async_remote_copy(
                 src_ref=src.at[side % 2, peer, at],
                 dst_ref=dst.at[side % 2, me, at],
@@ -225,18 +226,21 @@
             g_out[0, j, at, :] = side_by_side(early, swapped(late)).astype(BF16)
             g_out[1, j, at, :] = side_by_side(swapped(early), late).astype(BF16)
 
-    feature_chunk(chunks - 2)
-    feature_chunk(chunks - 1)
-    spread(g_out, u_in, 0, 1, wide)
-    feature_chunk(1)
+        spread(g_out, u_in, 0, q, part)
+
+    @pl.loop(1, chunks)
+    def _(q):
+        feature_chunk(q)
 
     @pl.when(me > 0)
     def _():
         halo_kv.wait_recv()
 
     feature_chunk(0)
-    spread(g_out, u_in, 0, 0, wide)
-    spread(g_out, u_in, 1, 0, packed)
+
+    @pl.loop(0, 2)
+    def _(q):
+        spread(g_out, u_in, 1, q, wide)
 
     @pl.when(me < groups - 1)
     def _():
@@ -344,8 +348,8 @@
 
             spread(v_out, f_in, 2 + side, q, back)
 
-    convolve(0, wide, packed)
-    convolve(1, packed, part)
+    convolve(0, part, wide)
+    convolve(1, wide, part)
 
     loads[5].wait()
 
@@ -377,7 +381,8 @@
             device_id_type=MESH_ID,
         )
 
-    await_chunk(f_in, 2, 0, packed)
+    for q in range(packed // wide):
+        await_chunk(f_in, 2, q, wide)
 
     @pl.loop(0, chunks)
     def _(q):

time: 70.6 us -> 69.8 us (0.989)
    pallas_call x1, Pallas kernels: 68.5 us -> 67.8 us  [fused(): pl.pallas_call(functools.partial(fused_kernel, groups, rows), out_shape=j...]
where the time goes in v5:
time: 69.8 us; the launch traced here: 69.6 us
  Pallas kernels  67.8 us (97%)
  local copies, waits for them, and re-layouts  1.87 us (3%)
    pallas_call x1, Pallas kernels, fused(): pl.pallas_call(functools.partial(fused_kernel, groups, rows), out_shape=j...  67.8 us
    unnamed x1, local copies, waits for them, and re-layouts  1.87 us

profile of v5, /device:TPU:0, one launch (start us, length us, event | category | flops | bytes accessed | tf_op | source)
XLA Modules:
  0.0 69.6 jit_solution(5393377178254781647)
XLA Ops:
  0.0 67.8 %shard_map.100 = bf16[256,1024]{1,0:T(8,128)(2,1)} custom-call(bf16[3,256,2048]{2,1,0:T(8,128)(2,1)} %proj.1, f32[3,7,2048]{2,1,0:T(8,128)} %taps.1, f32[128,4096]{1,0:T(8,128)} %filt.1, f32[1,128]{1,0:T(1,128)} %bitcast.1, bf16[2048,2048]{1,0:T(8,128)(2,1)} %weights.1, f32[16,16]{1,0:T(8,128)} %scales.1, bf16[16,640,256]{2,1,0:T(8,128)(2,1)} %constant.8.clone.t_first, ...), custom_call_target="tpu_custom_call" | custom-call | flops 10000000000 | bytes 33554432 | tf_op jit(solution)/shard_map/pallas_call | solution.py:433
  67.8 1.9 %copy.12 = bf16[256,1024]{1,0:T(8,128)(2,1)} copy(bf16[256,1024]{1,0:T(8,128)(2,1)} %shard_map.100) | data formatting | bytes 1048576

commit v6 on v1

--- a/solution.py
+++ b/solution.py
@@ -113,18 +113,21 @@
     pl.semaphore_signal(barrier, inc=1, device_id=(me, other), device_id_type=MESH_ID)
     pl.semaphore_wait(barrier, groups)
 
-    halo = pltpu.make_async_remote_copy(
-        src_ref=proj.at[:, pl.ds(rows - RIM, RIM)],
-        dst_ref=pb.at[:, pl.ds(0, RIM)],
-        send_sem=halo_sem.at[0],
-        recv_sem=halo_sem.at[1],
-        device_id=(lax.rem(me + 1, groups), mine),
-        device_id_type=MESH_ID,
-    )
+    def halo(first, count, slot):
+        return pltpu.make_async_remote_copy(
+            src_ref=proj.at[pl.ds(first, count), pl.ds(rows - RIM, RIM)],
+            dst_ref=pb.at[pl.ds(first, count), pl.ds(0, RIM)],
+            send_sem=halo_sem.at[slot],
+            recv_sem=halo_sem.at[slot + 1],
+            device_id=(lax.rem(me + 1, groups), mine),
+            device_id_type=MESH_ID,
+        )
+
+    halo_kv, halo_q = halo(1, 2, 0), halo(0, 1, 2)
 
     @pl.when(me < groups - 1)
     def _():
-        halo.start()
+        halo_kv.start()
 
     @pl.when(me == 0)
     def _():
@@ -193,17 +196,21 @@
 
     @pl.when(me > 0)
     def _():
-        halo.wait_recv()
+        halo_kv.wait_recv()
 
     feature_chunk(0)
 
+    @pl.when(me < groups - 1)
+    def _():
+        halo_q.start()
+
     loads[0].wait()
 
-    @pl.loop(0, groups)
+    @pl.loop(0, groups, unroll=4)
     def _(a):
         for part in range(rows // LANES):
             start = pl.multiple_of(a * rows + part * LANES, LANES)
-            ft[a, part * LANES : (part + 1) * LANES, :] = fl[:, pl.ds(start, LANES)].T.astype(BF16)
+            ft[a, part * LANES : (part + 1) * LANES, :] = fl[:, pl.ds(start, LANES)].astype(BF16).T
 
     for load in loads[1:5]:
         load.wait()
@@ -221,29 +228,12 @@
         right = x1[pl.ds(4 * j + 2, 2)].reshape(2 * rows, LANES)
         return jnp.concatenate([left, right], axis=1)
 
-    @pl.loop(0, rows // SUB)
+    @pl.loop(0, rows // SUB, unroll=4)
     def _(s):
         first_stage(ft, s)
 
-    @pl.loop(0, pairs)
-    def _(j):
+    for j in range(pairs):
         spec[j] = dot(m_ahead[...], pair_of(j))
-
-    loads[5].wait()
-    cuts = w.shape[1] // BLK
-
-    @pl.loop(0, w.shape[0] // BLK)
-    def _(b):
-        at = pl.ds(pl.multiple_of(b * BLK, BLK), BLK)
-        for n in range(cuts):
-            cols = slice(n * BLK, (n + 1) * BLK)
-            w[at, cols] = (w[at, cols].astype(F32) * scales[b, n]).astype(BF16)
-
-    @pl.loop(0, chunks)
-    def _(q):
-        @pl.loop(0, groups)
-        def _(j):
-            feat_q[j, rows_of(q), :] = featured(0, q, j)
 
     per_chunk = CHUNK // SUB
 
@@ -252,12 +242,11 @@
         q = lax.rem(i + 1, chunks)
         await_chunk(u_in, q, recv_u)
 
-        @pl.loop(0, per_chunk)
+        @pl.loop(0, per_chunk, unroll=per_chunk)
         def _(s):
             first_stage(u_in, q * per_chunk + s)
 
-    @pl.loop(0, pairs)
-    def _(j):
+    for j in range(pairs):
         values = dot(m_ahead[...], pair_of(j))
         re_u, im_u = values[:rows], values[rows:]
         re_h, im_h = spec[j, 0:rows, :], spec[j, rows : 2 * rows, :]
@@ -270,7 +259,7 @@
 
     @pl.loop(0, chunks)
     def _(q):
-        @pl.loop(0, per_chunk)
+        @pl.loop(0, per_chunk, unroll=per_chunk)
         def _(i):
             s = q * per_chunk + i
             at = pl.ds(pl.multiple_of(s * SUB, SUB), SUB)
@@ -279,6 +268,27 @@
             v_out[:, at, :] = (conv + direct).astype(BF16).reshape(groups, SUB, LANES)
 
         spread(v_out, f_in, q, 1)
+
+    loads[5].wait()
+    cuts = w.shape[1] // BLK
+
+    @pl.loop(0, w.shape[0] // BLK)
+    def _(b):
+        at = pl.ds(pl.multiple_of(b * BLK, BLK), BLK)
+        for n in range(cuts):
+            cols = slice(n * BLK, (n + 1) * BLK)
+            scale = jnp.full((BLK, BLK), scales[b, n], F32).astype(BF16)
+            w[at, cols] = w[at, cols] * scale
+
+    @pl.when(me > 0)
+    def _():
+        halo_q.wait_recv()
+
+    @pl.loop(0, chunks)
+    def _(q):
+        @pl.loop(0, groups, unroll=4)
+        def _(j):
+            feat_q[j, rows_of(q), :] = featured(0, q, j)
 
     def swap(q):
         return pltpu.make_async_remote_copy(
@@ -310,7 +320,8 @@
 
     @pl.when(me < groups - 1)
     def _():
-        halo.wait_send()
+        halo_kv.wait_send()
+        halo_q.wait_send()
 
     sent = g_out.at[pl.ds(0, groups - 1)]
     pltpu.make_async_copy(sent, sent, send_sem.at[0]).wait()
@@ -357,7 +368,7 @@
             pltpu.VMEM((rows, half), BF16),
             pltpu.VMEM((rows, half), BF16),
             pltpu.SemaphoreType.DMA((7,)),
-            pltpu.SemaphoreType.DMA((2,)),
+            pltpu.SemaphoreType.DMA((4,)),
             pltpu.SemaphoreType.DMA((3,)),
             pltpu.SemaphoreType.DMA((chunks,)),
             pltpu.SemaphoreType.DMA((chunks,)),

time: 73.8 us -> 68.2 us (0.924)
  Pallas kernels: 71.7 us -> 66.1 us
    pallas_call x1, Pallas kernels: 71.7 us -> 66.1 us  [fused(): pl.pallas_call(functools.partial(fused_kernel, groups, rows), out_shape=j...]
where the time goes in v6:
time: 68.2 us; the launch traced here: 68 us
  Pallas kernels  66.1 us (97%)
  local copies, waits for them, and re-layouts  1.87 us (3%)
    pallas_call x1, Pallas kernels, fused(): pl.pallas_call(functools.partial(fused_kernel, groups, rows), out_shape=j...  66.1 us
    unnamed x1, local copies, waits for them, and re-layouts  1.87 us

profile of v6, /device:TPU:0, one launch (start us, length us, event | category | flops | bytes accessed | tf_op | source)
XLA Modules:
  0.0 68.0 jit_solution(3609231362457725361)
XLA Ops:
  0.0 66.1 %shard_map.100 = bf16[256,1024]{1,0:T(8,128)(2,1)} custom-call(bf16[3,256,2048]{2,1,0:T(8,128)(2,1)} %proj.1, f32[3,7,2048]{2,1,0:T(8,128)} %taps.1, f32[128,4096]{1,0:T(8,128)} %filt.1, f32[1,128]{1,0:T(1,128)} %bitcast.1, bf16[2048,2048]{1,0:T(8,128)(2,1)} %weights.1, f32[16,16]{1,0:T(8,128)} %scales.1, bf16[16,576,256]{2,1,0:T(8,128)(2,1)} %constant.8.clone.t_first, ...), custom_call_target="tpu_custom_call" | custom-call | flops 10000000000 | bytes 33554432 | tf_op jit(solution)/shard_map/pallas_call | solution.py:345
  66.1 1.9 %copy.12 = bf16[256,1024]{1,0:T(8,128)(2,1)} copy(bf16[256,1024]{1,0:T(8,128)(2,1)} %shard_map.100) | data formatting | bytes 1048576

commit v7 on v6

--- a/solution.py
+++ b/solution.py
@@ -49,6 +49,11 @@
     return [x.astype(ml_dtypes.bfloat16) for x in (first, ahead, back, last)]
 
 
+def return_pieces(rows):
+    sizes = [CHUNK] * (rows // CHUNK - 1) + [CHUNK // 2] * 2
+    return [(sum(sizes[:i]), size) for i, size in enumerate(sizes)]
+
+
 def dot(a, b):
     return jnp.dot(a, b, preferred_element_type=F32)
 
@@ -57,7 +62,7 @@
     groups,
     rows,
     proj,
-    taps,
+    taps_hbm,
     filt,
     gain,
     weights,
@@ -68,6 +73,9 @@
     t_last,
     out,
     pb,
+    taps,
+    rim_out,
+    rim_in,
     g_out,
     u_in,
     v_out,
@@ -102,6 +110,8 @@
 
     load_k = pltpu.make_async_copy(proj, pb.at[:, pl.ds(RIM, rows)], loc_sem.at[0])
     load_k.start()
+    load_taps = pltpu.make_async_copy(taps_hbm, taps, loc_sem.at[7])
+    load_taps.start()
 
     barrier = pltpu.get_barrier_semaphore()
 
@@ -113,27 +123,33 @@
     pl.semaphore_signal(barrier, inc=1, device_id=(me, other), device_id_type=MESH_ID)
     pl.semaphore_wait(barrier, groups)
 
-    def halo(first, count, slot):
+    def halo(src, dst, slot):
         return pltpu.make_async_remote_copy(
-            src_ref=proj.at[pl.ds(first, count), pl.ds(rows - RIM, RIM)],
-            dst_ref=pb.at[pl.ds(first, count), pl.ds(0, RIM)],
+            src_ref=src,
+            dst_ref=dst,
             send_sem=halo_sem.at[slot],
             recv_sem=halo_sem.at[slot + 1],
             device_id=(lax.rem(me + 1, groups), mine),
             device_id_type=MESH_ID,
         )
 
-    halo_kv, halo_q = halo(1, 2, 0), halo(0, 1, 2)
-
-    @pl.when(me < groups - 1)
-    def _():
-        halo_kv.start()
+    halo_kv = halo(rim_out, rim_in, 0)
+    halo_q = halo(proj.at[0, pl.ds(rows - RIM, RIM)], pb.at[0, pl.ds(0, RIM)], 2)
 
     @pl.when(me == 0)
     def _():
         pb[:, 0:RIM, :] = jnp.zeros((pb.shape[0], RIM, pb.shape[2]), BF16)
 
     load_k.wait()
+    few = RIM // 2
+
+    @pl.when(me < groups - 1)
+    def _():
+        ends = [pb[p, rows : rows + RIM, :].astype(F32)[few:] for p in (1, 2)]
+        rim_out[...] = jnp.concatenate(ends, axis=0).astype(BF16)
+        halo_kv.start()
+
+    load_taps.wait()
     loads = [
         pltpu.make_async_copy(src, dst, loc_sem.at[1 + i])
         for i, (src, dst) in enumerate(
@@ -162,23 +178,23 @@
     def rows_of(q):
         return pl.ds(pl.multiple_of(q * CHUNK, CHUNK), CHUNK)
 
-    def spread(src, dst, q, recv):
+    def spread(src, dst, at, q, recv):
         @pl.loop(1, groups)
         def _(step):
             peer = lax.rem(me + step, groups)
             pltpu.make_async_remote_copy(
-                src_ref=src.at[peer, rows_of(q)],
-                dst_ref=dst.at[me, rows_of(q)],
+                src_ref=src.at[peer, at],
+                dst_ref=dst.at[me, at],
                 send_sem=send_sem.at[recv],
                 recv_sem=(recv_u if recv == 0 else recv_f).at[q],
                 device_id=(peer, mine),
                 device_id_type=MESH_ID,
             ).start()
 
-        dst[me, rows_of(q), :] = src[me, rows_of(q), :]
-
-    def await_chunk(dst, q, sem):
-        view = dst.at[pl.ds(0, groups - 1), rows_of(q)]
+        dst[me, at, :] = src[me, at, :]
+
+    def await_chunk(dst, at, q, sem):
+        view = dst.at[pl.ds(0, groups - 1), at]
         pltpu.make_async_copy(view, view, sem.at[q]).wait()
 
     def feature_chunk(q):
@@ -188,7 +204,7 @@
             v = featured(2, q, j).astype(F32)
             g_out[j, rows_of(q), :] = (k * v).astype(BF16)
 
-        spread(g_out, u_in, q, 0)
+        spread(g_out, u_in, rows_of(q), q, 0)
 
     @pl.loop(1, chunks)
     def _(q):
@@ -197,12 +213,13 @@
     @pl.when(me > 0)
     def _():
         halo_kv.wait_recv()
+        both = rim_in[...].astype(F32)
+        blank = jnp.zeros((few, pb.shape[2]), F32)
+        for p in (1, 2):
+            own = both[(p - 1) * few : p * few]
+            pb[p, 0:RIM, :] = jnp.concatenate([blank, own], axis=0).astype(BF16)
 
     feature_chunk(0)
-
-    @pl.when(me < groups - 1)
-    def _():
-        halo_q.start()
 
     loads[0].wait()
 
@@ -240,11 +257,15 @@
     @pl.loop(0, chunks)
     def _(i):
         q = lax.rem(i + 1, chunks)
-        await_chunk(u_in, q, recv_u)
+        await_chunk(u_in, rows_of(q), q, recv_u)
 
         @pl.loop(0, per_chunk, unroll=per_chunk)
         def _(s):
             first_stage(u_in, q * per_chunk + s)
+
+    @pl.when(me < groups - 1)
+    def _():
+        halo_q.start()
 
     for j in range(pairs):
         values = dot(m_ahead[...], pair_of(j))
@@ -257,17 +278,14 @@
         x1[pl.ds(4 * j, 2)] = z[:, :LANES].reshape(2, rows, LANES)
         x1[pl.ds(4 * j + 2, 2)] = z[:, LANES:].reshape(2, rows, LANES)
 
-    @pl.loop(0, chunks)
-    def _(q):
-        @pl.loop(0, per_chunk, unroll=per_chunk)
-        def _(i):
-            s = q * per_chunk + i
-            at = pl.ds(pl.multiple_of(s * SUB, SUB), SUB)
+    pieces = return_pieces(rows)
+    for q, (start, count) in enumerate(pieces):
+        for s in range(start // SUB, (start + count) // SUB):
+            at = pl.ds(s * SUB, SUB)
             conv = dot(m_last[s], x1[:, at, :].reshape(slabs * SUB, LANES))
             direct = gain[...] * u_in[:, at, :].reshape(groups * SUB, LANES).astype(F32)
             v_out[:, at, :] = (conv + direct).astype(BF16).reshape(groups, SUB, LANES)
-
-        spread(v_out, f_in, q, 1)
+        spread(v_out, f_in, pl.ds(start, count), q, 1)
 
     loads[5].wait()
     cuts = w.shape[1] // BLK
@@ -290,33 +308,33 @@
         def _(j):
             feat_q[j, rows_of(q), :] = featured(0, q, j)
 
-    def swap(q):
+    def swap(q, at):
         return pltpu.make_async_remote_copy(
-            src_ref=part_out.at[rows_of(q)],
-            dst_ref=part_in.at[rows_of(q)],
+            src_ref=part_out.at[at],
+            dst_ref=part_in.at[at],
             send_sem=send_sem.at[2],
             recv_sem=recv_p.at[q],
             device_id=(me, other),
             device_id_type=MESH_ID,
         )
 
-    @pl.loop(0, chunks)
-    def _(q):
-        await_chunk(f_in, q, recv_f)
+    theirs = pl.ds(pl.multiple_of(other * half, half), half)
+    ours = pl.ds(pl.multiple_of(mine * half, half), half)
+    for q, (start, count) in enumerate(pieces):
+        at = pl.ds(start, count)
+        await_chunk(f_in, at, q, recv_f)
         for j in range(groups):
-            product = feat_q[j, rows_of(q), :].astype(F32) * f_in[j, rows_of(q), :].astype(F32)
-            gated[:, j * LANES : (j + 1) * LANES] = product.astype(BF16)
-        theirs = pl.ds(pl.multiple_of(other * half, half), half)
-        ours = pl.ds(pl.multiple_of(mine * half, half), half)
-        part_out[rows_of(q), :] = dot(gated[...], w[:, theirs]).astype(BF16)
-        swap(q).start()
-        part_own[rows_of(q), :] = dot(gated[...], w[:, ours]).astype(BF16)
-
-    @pl.loop(0, chunks)
-    def _(q):
-        swap(q).wait_recv()
-        total = part_own[rows_of(q), :].astype(F32) + part_in[rows_of(q), :].astype(F32)
-        out[rows_of(q), :] = total.astype(BF16)
+            product = feat_q[j, at, :].astype(F32) * f_in[j, at, :].astype(F32)
+            gated[0:count, j * LANES : (j + 1) * LANES] = product.astype(BF16)
+        part_out[at, :] = dot(gated[0:count, :], w[:, theirs]).astype(BF16)
+        swap(q, at).start()
+        part_own[at, :] = dot(gated[0:count, :], w[:, ours]).astype(BF16)
+
+    for q, (start, count) in enumerate(pieces):
+        at = pl.ds(start, count)
+        swap(q, at).wait_recv()
+        total = part_own[at, :].astype(F32) + part_in[at, :].astype(F32)
+        out[at, :] = total.astype(BF16)
 
     @pl.when(me < groups - 1)
     def _():
@@ -345,10 +363,13 @@
     return pl.pallas_call(
         functools.partial(fused_kernel, groups, rows),
         out_shape=jax.ShapeDtypeStruct((rows, half), BF16),
-        in_specs=[hbm, vmem, hbm, vmem, hbm, smem, hbm, hbm, hbm, hbm],
+        in_specs=[hbm, hbm, hbm, vmem, hbm, smem, hbm, hbm, hbm, hbm],
         out_specs=vmem,
         scratch_shapes=[
             pltpu.VMEM((3, RIM + rows, local_ch), BF16),
+            pltpu.VMEM(feat_weight.shape, F32),
+            pltpu.VMEM((RIM, local_ch), BF16),
+            pltpu.VMEM((RIM, local_ch), BF16),
             block,
             block,
             block,
@@ -367,12 +388,12 @@
             pltpu.VMEM((rows, half), BF16),
             pltpu.VMEM((rows, half), BF16),
             pltpu.VMEM((rows, half), BF16),
-            pltpu.SemaphoreType.DMA((7,)),
+            pltpu.SemaphoreType.DMA((8,)),
             pltpu.SemaphoreType.DMA((4,)),
             pltpu.SemaphoreType.DMA((3,)),
             pltpu.SemaphoreType.DMA((chunks,)),
-            pltpu.SemaphoreType.DMA((chunks,)),
-            pltpu.SemaphoreType.DMA((chunks,)),
+            pltpu.SemaphoreType.DMA((len(return_pieces(rows)),)),
+            pltpu.SemaphoreType.DMA((len(return_pieces(rows)),)),
         ],
         compiler_params=pltpu.CompilerParams(
             collective_id=0, has_side_effects=True, vmem_limit_bytes=58 * 2**20

time: 68.2 us -> 68.1 us (level)
  no operation moved by 1% of the time
where the time goes in v7:
time: 68.1 us; the launch traced here: 67.9 us
  Pallas kernels  66 us (97%)
  local copies, waits for them, and re-layouts  1.87 us (3%)
    pallas_call x1, Pallas kernels, fused(): pl.pallas_call(functools.partial(fused_kernel, groups, rows), out_shape=j...  66 us
    unnamed x1, local copies, waits for them, and re-layouts  1.87 us

profile of v7, /device:TPU:0, one launch (start us, length us, event | category | flops | bytes accessed | tf_op | source)
XLA Modules:
  0.0 67.9 jit_solution(3154032452114247783)
XLA Ops:
  0.0 66.0 %shard_map.100 = bf16[256,1024]{1,0:T(8,128)(2,1)} custom-call(bf16[3,256,2048]{2,1,0:T(8,128)(2,1)} %proj.1, f32[3,7,2048]{2,1,0:T(8,128)} %taps_hbm.1, f32[128,4096]{1,0:T(8,128)} %filt.1, f32[1,128]{1,0:T(1,128)} %bitcast.1, bf16[2048,2048]{1,0:T(8,128)(2,1)} %weights.1, f32[16,16]{1,0:T(8,128)} %scales.1, bf16[16,576,256]{2,1,0:T(8,128)(2,1)} %constant.8.clone.t_first, ...), custom_call_target="tpu_custom_call" | custom-call | flops 10000000000 | bytes 33554432 | tf_op jit(solution)/shard_map/pallas_call | solution.py:363
  66.0 1.9 %copy.12 = bf16[256,1024]{1,0:T(8,128)(2,1)} copy(bf16[256,1024]{1,0:T(8,128)(2,1)} %shard_map.100) | data formatting | bytes 1048576

commit v8 on v7

--- a/solution.py
+++ b/solution.py
@@ -50,8 +50,11 @@
 
 
 def return_pieces(rows):
-    sizes = [CHUNK] * (rows // CHUNK - 1) + [CHUNK // 2] * 2
-    return [(sum(sizes[:i]), size) for i, size in enumerate(sizes)]
+    return [(start, CHUNK) for start in range(0, rows, CHUNK)]
+
+
+def projected_pieces(rows):
+    return [(0, rows // 2)] + [(start, CHUNK) for start in range(rows // 2, rows, CHUNK)]
 
 
 def dot(a, b):
@@ -252,6 +255,17 @@
     for j in range(pairs):
         spec[j] = dot(m_ahead[...], pair_of(j))
 
+    loads[5].wait()
+    cuts = w.shape[1] // BLK
+
+    @pl.loop(0, w.shape[0] // BLK)
+    def _(b):
+        at = pl.ds(pl.multiple_of(b * BLK, BLK), BLK)
+        for n in range(cuts):
+            cols = slice(n * BLK, (n + 1) * BLK)
+            scale = jnp.full((BLK, BLK), scales[b, n], F32).astype(BF16)
+            w[at, cols] = w[at, cols] * scale
+
     per_chunk = CHUNK // SUB
 
     @pl.loop(0, chunks)
@@ -287,17 +301,6 @@
             v_out[:, at, :] = (conv + direct).astype(BF16).reshape(groups, SUB, LANES)
         spread(v_out, f_in, pl.ds(start, count), q, 1)
 
-    loads[5].wait()
-    cuts = w.shape[1] // BLK
-
-    @pl.loop(0, w.shape[0] // BLK)
-    def _(b):
-        at = pl.ds(pl.multiple_of(b * BLK, BLK), BLK)
-        for n in range(cuts):
-            cols = slice(n * BLK, (n + 1) * BLK)
-            scale = jnp.full((BLK, BLK), scales[b, n], F32).astype(BF16)
-            w[at, cols] = w[at, cols] * scale
-
     @pl.when(me > 0)
     def _():
         halo_q.wait_recv()
@@ -320,9 +323,12 @@
 
     theirs = pl.ds(pl.multiple_of(other * half, half), half)
     ours = pl.ds(pl.multiple_of(mine * half, half), half)
-    for q, (start, count) in enumerate(pieces):
+    groups_of_rows = projected_pieces(rows)
+    for q, (start, count) in enumerate(groups_of_rows):
         at = pl.ds(start, count)
-        await_chunk(f_in, at, q, recv_f)
+        for i, (low, size) in enumerate(pieces):
+            if start <= low < start + count:
+                await_chunk(f_in, pl.ds(low, size), i, recv_f)
         for j in range(groups):
             product = feat_q[j, at, :].astype(F32) * f_in[j, at, :].astype(F32)
             gated[0:count, j * LANES : (j + 1) * LANES] = product.astype(BF16)
@@ -330,7 +336,7 @@
         swap(q, at).start()
         part_own[at, :] = dot(gated[0:count, :], w[:, ours]).astype(BF16)
 
-    for q, (start, count) in enumerate(pieces):
+    for q, (start, count) in enumerate(groups_of_rows):
         at = pl.ds(start, count)
         swap(q, at).wait_recv()
         total = part_own[at, :].astype(F32) + part_in[at, :].astype(F32)
@@ -384,7 +390,7 @@
             pltpu.VMEM(tables[2].shape, BF16),
             pltpu.VMEM(tables[3].shape, BF16),
             pltpu.VMEM(out_values.shape, BF16),
-            pltpu.VMEM((CHUNK, local_ch), BF16),
+            pltpu.VMEM((rows // 2, local_ch), BF16),
             pltpu.VMEM((rows, half), BF16),
             pltpu.VMEM((rows, half), BF16),
             pltpu.VMEM((rows, half), BF16),
@@ -393,7 +399,7 @@
             pltpu.SemaphoreType.DMA((3,)),
             pltpu.SemaphoreType.DMA((chunks,)),
             pltpu.SemaphoreType.DMA((len(return_pieces(rows)),)),
-            pltpu.SemaphoreType.DMA((len(return_pieces(rows)),)),
+            pltpu.SemaphoreType.DMA((len(projected_pieces(rows)),)),
         ],
         compiler_params=pltpu.CompilerParams(
             collective_id=0, has_side_effects=True, vmem_limit_bytes=58 * 2**20

time: 68.1 us -> 69.4 us (1.019)
  the two profiles are of different devices: /device:TPU:0 before, /device:TPU:26 now
where the time goes in v8:
time: 69.4 us; the launch traced here: 69.2 us
  Pallas kernels  67.3 us (97%)
  local copies, waits for them, and re-layouts  1.87 us (3%)
    pallas_call x1, Pallas kernels, fused(): pl.pallas_call(functools.partial(fused_kernel, groups, rows), out_shape=j...  67.3 us
    unnamed x1, local copies, waits for them, and re-layouts  1.87 us

profile of v8, /device:TPU:26, one launch (start us, length us, event | category | flops | bytes accessed | tf_op | source)
XLA Modules:
  0.0 69.2 jit_solution(749552935807750871)
XLA Ops:
  0.0 67.3 %shard_map.100 = bf16[256,1024]{1,0:T(8,128)(2,1)} custom-call(bf16[3,256,2048]{2,1,0:T(8,128)(2,1)} %proj.1, f32[3,7,2048]{2,1,0:T(8,128)} %taps_hbm.1, f32[128,4096]{1,0:T(8,128)} %filt.1, f32[1,128]{1,0:T(1,128)} %bitcast.1, bf16[2048,2048]{1,0:T(8,128)(2,1)} %weights.1, f32[16,16]{1,0:T(8,128)} %scales.1, bf16[16,576,256]{2,1,0:T(8,128)(2,1)} %constant.8.clone.t_first, ...), custom_call_target="tpu_custom_call" | custom-call | flops 10000000000 | bytes 33554432 | tf_op jit(solution)/shard_map/pallas_call | solution.py:369
  67.3 1.9 %copy.12 = bf16[256,1024]{1,0:T(8,128)(2,1)} copy(bf16[256,1024]{1,0:T(8,128)(2,1)} %shard_map.100) | data formatting | bytes 1048576

commit v9 on v8

--- a/solution.py
+++ b/solution.py
@@ -255,17 +255,6 @@
     for j in range(pairs):
         spec[j] = dot(m_ahead[...], pair_of(j))
 
-    loads[5].wait()
-    cuts = w.shape[1] // BLK
-
-    @pl.loop(0, w.shape[0] // BLK)
-    def _(b):
-        at = pl.ds(pl.multiple_of(b * BLK, BLK), BLK)
-        for n in range(cuts):
-            cols = slice(n * BLK, (n + 1) * BLK)
-            scale = jnp.full((BLK, BLK), scales[b, n], F32).astype(BF16)
-            w[at, cols] = w[at, cols] * scale
-
     per_chunk = CHUNK // SUB
 
     @pl.loop(0, chunks)
@@ -300,6 +289,17 @@
             direct = gain[...] * u_in[:, at, :].reshape(groups * SUB, LANES).astype(F32)
             v_out[:, at, :] = (conv + direct).astype(BF16).reshape(groups, SUB, LANES)
         spread(v_out, f_in, pl.ds(start, count), q, 1)
+
+    loads[5].wait()
+    cuts = w.shape[1] // BLK
+
+    @pl.loop(0, w.shape[0] // BLK)
+    def _(b):
+        at = pl.ds(pl.multiple_of(b * BLK, BLK), BLK)
+        for n in range(cuts):
+            cols = slice(n * BLK, (n + 1) * BLK)
+            scale = jnp.full((BLK, BLK), scales[b, n], F32).astype(BF16)
+            w[at, cols] = w[at, cols] * scale
 
     @pl.when(me > 0)
     def _():

time: 69.4 us -> 69.4 us (level)
  no operation moved by 1% of the time
where the time goes in v9:
time: 69.4 us; the launch traced here: 69.2 us
  Pallas kernels  67.3 us (97%)
  local copies, waits for them, and re-layouts  1.87 us (3%)
    pallas_call x1, Pallas kernels, fused(): pl.pallas_call(functools.partial(fused_kernel, groups, rows), out_shape=j...  67.3 us
    unnamed x1, local copies, waits for them, and re-layouts  1.87 us

profile of v9, /device:TPU:26, one launch (start us, length us, event | category | flops | bytes accessed | tf_op | source)
XLA Modules:
  0.0 69.2 jit_solution(15944697089488584552)
XLA Ops:
  0.0 67.3 %shard_map.100 = bf16[256,1024]{1,0:T(8,128)(2,1)} custom-call(bf16[3,256,2048]{2,1,0:T(8,128)(2,1)} %proj.1, f32[3,7,2048]{2,1,0:T(8,128)} %taps_hbm.1, f32[128,4096]{1,0:T(8,128)} %filt.1, f32[1,128]{1,0:T(1,128)} %bitcast.1, bf16[2048,2048]{1,0:T(8,128)(2,1)} %weights.1, f32[16,16]{1,0:T(8,128)} %scales.1, bf16[16,576,256]{2,1,0:T(8,128)(2,1)} %constant.8.clone.t_first, ...), custom_call_target="tpu_custom_call" | custom-call | flops 10000000000 | bytes 33554432 | tf_op jit(solution)/shard_map/pallas_call | solution.py:369
  67.3 1.9 %copy.12 = bf16[256,1024]{1,0:T(8,128)(2,1)} copy(bf16[256,1024]{1,0:T(8,128)(2,1)} %shard_map.100) | data formatting | bytes 1048576
